TPU v7x, 32 devices: a whole 2x2x4 slice. The times are simulated.
32 devices in a mesh: grp: 2 (over y), tile: 16 (over z, x, core).
Axes of the slice: x: 2, y: 2, z: 4, core: 2. Of those that a mesh axis runs over, the one named last changes fastest.
Arguments:
- first_feat: bfloat16 [448, 128, 256], P(('grp', 'tile')), parts along dimension 0, may hold values from -4 to 4
- second_feat: bfloat16 [448, 128, 256], P(('grp', 'tile')), parts along dimension 0, may hold values from -4 to 4
- hidden_init: bfloat16 [448, 128, 256], P(('grp', 'tile')), parts along dimension 0, may hold values from -4 to 4
- cotangent: bfloat16 [448, 128, 256], P(('grp', 'tile')), parts along dimension 0, may hold values from -6 to 6
- search_list: int32 [448, 4], P(('grp', 'tile')), parts along dimension 0, may hold values from 1 to 222, as said below
- offsets: int32 [2, 448], P(None, ('grp', 'tile')), parts along dimension 1, may hold values from -1 to 1
- lengths: int32 [448], P(('grp', 'tile')), parts along dimension 0, may hold values from 1 to 4
- hid_weight: bfloat16 [256, 512], replicated, may hold values from -0.375 to 0.375
- in_weight: bfloat16 [256, 768], replicated, may hold values from -0.375 to 0.375
- cand_weight: bfloat16 [256, 256], replicated, may hold values from -0.375 to 0.375
- disp_weight: float32 [2, 768], replicated, may hold values from -1.5 to 1.5
- gate_bias: float32 [768], replicated, may hold values from -1 to 1
Outputs:
- hidden_state: float32 [448, 128, 256], P(('grp', 'tile')), parts along dimension 0
- flow: float32 [448, 2, 128], P(('grp', 'tile')), parts along dimension 0
- grad_second: float32 [448, 128, 256], P(('grp', 'tile')), parts along dimension 0
There are 2 independent parts, one for each index of `grp`. A program takes and returns all parts, laid end to end along the dimension named above; an argument that names none is the same for every part. Nothing has to cross between parts.
Inputs may be any that keep to these rules, and one draw needn't show every extreme that they name: `search_list`: the 4 ids of a block are distinct, and each, plus any offset of that block, names a block whose row lies within one block row of the block's own row.
All inputs are finite; a program needn't handle non-finite values.
Results may differ from a plain program's by a relative error of at most 0.0073.
Values may be sent and summed in bfloat16 or wider, within the bound.
A program may use at most 128 MiB of HBM per device.

v0:
```python
import math

import jax
import jax.numpy as jnp
from jax import lax
from jax.sharding import PartitionSpec as P

PH = 8
PW = 16
BW = 7
ITERS = 2


def with_halo(value, sides, width):
    for axis, dim in sides:
        count, length = (lax.axis_size(axis), value.shape[dim])
        up = [(i, (i + 1) % count) for i in range(count - 1)]
        down = [(j, i) for i, j in up]
        last = lax.slice_in_dim(value, length - width, length, axis=dim)
        initial = lax.slice_in_dim(value, 0, width, axis=dim)
        before = lax.ppermute(last, axis, up)
        after = lax.ppermute(initial, axis, down)
        value = jnp.concatenate([before, value, after], axis=dim)
    return value


def passed_along(block, axis, distance):
    devices = range(lax.axis_size(axis))
    route = [(i - distance, i) for i in devices if i - distance in devices]
    return lax.ppermute(block, axis, route)


def motion_update(
    hidden,
    motion_half,
    flow_rows,
    flow_cols,
    hid_weight,
    in_weight,
    cand_weight,
    disp_weight,
    gate_bias,
):
    channels = hidden.shape[1]
    from_hidden = jnp.dot(
        hidden.astype(jnp.bfloat16), hid_weight, preferred_element_type=jnp.float32
    )
    from_input = jnp.dot(motion_half, in_weight, preferred_element_type=jnp.float32)
    inputs = (
        from_input
        + flow_rows[:, None] * disp_weight[0]
        + flow_cols[:, None] * disp_weight[1]
        + gate_bias
    )
    update = jax.nn.sigmoid(from_hidden[:, :channels] + inputs[:, :channels])
    reset_gate = jax.nn.sigmoid(from_hidden[:, channels:] + inputs[:, channels : 2 * channels])
    candidate = jnp.tanh(
        jnp.dot(
            (reset_gate * hidden).astype(jnp.bfloat16),
            cand_weight,
            preferred_element_type=jnp.float32,
        )
        + inputs[:, 2 * channels :]
    )
    return (1.0 - update) * hidden + update * candidate


def displacement(weights, block_ids, global_ids, cell_count):
    cell_index = jnp.arange(cell_count, dtype=jnp.int32)
    key_row = ((block_ids // BW - global_ids[:, None] // BW) * PH)[:, :, None] + (cell_index // PW)[
        None, None, :
    ]
    key_col = ((block_ids % BW - global_ids[:, None] % BW) * PW)[:, :, None] + (cell_index % PW)[
        None, None, :
    ]
    key_y = key_row.astype(jnp.float32) / PH
    key_x = key_col.astype(jnp.float32) / PW
    flow_rows = (
        jnp.sum(weights * key_y[:, None], axis=(2, 3))
        - (cell_index // PW).astype(jnp.float32)[None, :] / PH
    )
    flow_cols = (
        jnp.sum(weights * key_x[:, None], axis=(2, 3))
        - (cell_index % PW).astype(jnp.float32)[None, :] / PW
    )
    return (flow_rows, flow_cols)


def attend(queries, key_blocks, live_slots, score_scale):
    scores = (
        jnp.einsum("bpc,blkc->bplk", queries, key_blocks, preferred_element_type=jnp.float32)
        * score_scale
    )
    scores = jnp.where(live_slots[:, None, :, None], scores, -jnp.inf)
    row_max = jnp.max(scores, axis=(2, 3), keepdims=True)
    exponent = jnp.exp(scores - row_max)
    weights = exponent / jnp.sum(exponent, axis=(2, 3), keepdims=True)
    half_weights = weights.astype(jnp.bfloat16)
    motion = jnp.einsum(
        "bplk,blkc->bpc", half_weights, key_blocks, preferred_element_type=jnp.float32
    )
    return (weights, half_weights, motion)


def local(
    first_feat,
    second_feat,
    hidden_init,
    cotangent,
    search_list,
    offsets,
    lengths,
    hid_weight,
    in_weight,
    cand_weight,
    disp_weight,
    gate_bias,
):
    blocks, cell_count, channels = first_feat.shape
    slot_count = search_list.shape[1]
    score_scale = 1.0 / math.sqrt(channels)
    own_first = lax.axis_index("tile") * blocks
    rim_width = BW
    window = with_halo(second_feat, (("tile", 0),), rim_width)
    global_ids = own_first + jnp.arange(blocks, dtype=jnp.int32)
    live_slots = jnp.arange(slot_count, dtype=jnp.int32)[None, :] < lengths[:, None]
    hidden = hidden_init.reshape(blocks * cell_count, channels).astype(jnp.float32)
    for refine in range(ITERS):
        block_ids = search_list + offsets[refine][:, None]
        local_ids = block_ids - own_first + rim_width
        key_blocks = window[local_ids]
        queries = (
            first_feat.astype(jnp.float32) + hidden.reshape(blocks, cell_count, channels)
        ).astype(jnp.bfloat16)
        weights, half_weights, motion = attend(queries, key_blocks, live_slots, score_scale)
        flow_rows, flow_cols = displacement(weights, block_ids, global_ids, cell_count)
        hidden = motion_update(
            hidden,
            motion.astype(jnp.bfloat16).reshape(blocks * cell_count, channels),
            flow_rows.reshape(-1),
            flow_cols.reshape(-1),
            hid_weight,
            in_weight,
            cand_weight,
            disp_weight,
            gate_bias,
        )
    weight_grad = jnp.einsum(
        "bpc,blkc->bplk", cotangent, key_blocks, preferred_element_type=jnp.float32
    )
    row_delta = jnp.sum(weights * weight_grad, axis=(2, 3), keepdims=True)
    dscore = (weights * (weight_grad - row_delta) * score_scale).astype(jnp.bfloat16)
    stacked = jnp.concatenate([half_weights, dscore], axis=1)
    sources = jnp.concatenate([cotangent, queries], axis=1)
    contrib = jnp.einsum("bplk,bpc->blkc", stacked, sources, preferred_element_type=jnp.float32)
    span_count = 2 * rim_width + blocks
    summed = jnp.zeros((span_count, cell_count, channels), jnp.float32)
    summed = summed.at[local_ids.reshape(-1)].add(
        contrib.reshape(blocks * slot_count, cell_count, channels)
    )
    lower_part = summed[:rim_width]
    upper_part = summed[rim_width + blocks :]
    own_grad = summed[rim_width : rim_width + blocks]
    from_next = passed_along(lower_part, "tile", -1)
    from_prev = passed_along(upper_part, "tile", 1)
    own_grad = own_grad.at[blocks - rim_width :].add(from_next)
    own_grad = own_grad.at[:rim_width].add(from_prev)
    flow_pair = jnp.stack([flow_rows, flow_cols], axis=1)
    return (hidden.reshape(blocks, cell_count, channels), flow_pair, own_grad)


def solution(mesh):
    placed = (
        P(("grp", "tile"), None, None),
        P(("grp", "tile"), None, None),
        P(("grp", "tile"), None, None),
        P(("grp", "tile"), None, None),
        P(("grp", "tile"), None),
        P(None, ("grp", "tile")),
        P(("grp", "tile")),
        P(),
        P(),
        P(),
        P(),
        P(),
    )
    return jax.shard_map(
        local,
        mesh=mesh,
        in_specs=placed,
        out_specs=(
            P(("grp", "tile"), None, None),
            P(("grp", "tile"), None, None),
            P(("grp", "tile"), None, None),
        ),
        check_vma=False,
    )
```

profile of v0, /device:TPU:1, one launch (start us, length us, event | category | flops | bytes accessed | tf_op | source)
XLA Modules:
  0.0 103.3 jit_solution(7550369930305116408)
XLA Ops:
  0.6 0.0 copy-start
  0.7 2.1 %fusion.76 = (bf16[7,128,256]{2,1,0:T(8,128)(2,1)}, bf16[7,128,256]{2,1,0:T(8,128)(2,1)S(1)}) fusion(bf16[14,128,256]{2,1,0:T(8,128)(2,1)} %param.17), kind=kLoop, calls=%fused_computation.145 | loop fusion | bytes 1835008 | tf_op jit(solution)/shard_map/slice | solution.py:20
  2.7 4.5 %collective-permute-start = (bf16[7,128,256]{2,1,0:T(8,128)(2,1)S(1)}, bf16[7,128,256]{2,1,0:T(8,128)(2,1)}, u32[]{:S(2)}, u32[]{:S(2)}) collective-permute-start(bf16[7,128,256]{2,1,0:T(8,128)(2,1)S(1)} %get-tuple-element.42), channel_id=1, source_target_pairs={{0,1},{1,2},{2,3},{3,4},{4,5},{5,6},{6,7},{7,8},{8,9},{9,10},{10,1... | collective-permute-start | bytes 1376264 | tf_op jit(solution)/shard_map/ppermute | solution.py:21
  7.3 1.9 %collective-permute-start.1 = (bf16[7,128,256]{2,1,0:T(8,128)(2,1)}, bf16[7,128,256]{2,1,0:T(8,128)(2,1)}, u32[]{:S(2)}, u32[]{:S(2)}) collective-permute-start(bf16[7,128,256]{2,1,0:T(8,128)(2,1)} %get-tuple-element.41), channel_id=1, source_target_pairs={{1,0},{2,1},{3,2},{4,3},{5,4},{6,5},{7,6},{8,7},{9,8},{10,9},{11,1... | collective-permute-start | bytes 1376264 | tf_op jit(solution)/shard_map/ppermute | solution.py:22
  9.2 0.7 iota_compare_fusion
  9.9 0.8 slice_bitcast_fusion.1
  10.7 0.7 subtract_add_fusion
  11.4 0.1 copy.28
  11.5 0.1 reshape.357
  11.6 0.1 copy.24
  11.7 0.1 reshape.349
  11.8 0.8 slice_reduce_fusion.1
  12.6 0.1 copy.30
  12.7 0.1 copy.26
  12.8 3.7 %fusion.77 = f32[1792,512]{1,0:T(8,128)} fusion(bf16[1792,256]{1,0:T(8,128)(2,1)} %bitcast.91, bf16[256,512]{1,0:T(8,128)(2,1)} %param.23), kind=kOutput, calls=%fused_computation.146 | convolution fusion | flops 469762048 | bytes 4849664 | tf_op jit(solution)/shard_map/dot_general | solution.py:45
  16.5 0.1 convert_multiply_fusion.3
  16.6 0.1 copy.31
  16.7 0.1 copy.27
  16.8 0.1 copy.32
  16.8 0.1 reshape.345
  16.9 0.1 convert_multiply_fusion.2
  17.1 1.0 %constant_dynamic-update-slice_fusion.2 = bf16[28,128,256]{2,1,0:T(8,128)(2,1)S(1)} fusion(bf16[7,128,256]{2,1,0:T(8,128)(2,1)} %collective-permute-done), kind=kLoop, calls=%fused_computation.101 | loop fusion | bytes 917504
  18.1 0.1 constant_dynamic-update-slice_fusion.1
  18.2 1.1 %constant_dynamic-update-slice_fusion = bf16[28,128,256]{2,1,0:T(8,128)(2,1)S(1)} fusion(bf16[28,128,256]{2,1,0:T(8,128)(2,1)S(1)} %constant_dynamic-update-slice_fusion.1, bf16[7,128,256]{2,1,0:T(8,128)(2,1)} %collective-permute-done.1), kind=kLoop, calls=%fused_computation.99 | loop fusion | bytes 917504 | tf_op jit(solution)/shard_map/concatenate | solution.py:23
  19.3 2.7 %gather_fusion.1 = bf16[56,128,256]{2,1,0:T(8,128)(2,1)} fusion(bf16[28,128,256]{2,1,0:T(8,128)(2,1)S(1)} %constant_dynamic-update-slice_fusion, s32[1024]{0:T(1024)S(1)} %pad_clamp_fusion), kind=kCustom, calls=%fused_computation.1 | custom fusion | bytes 7340256 | tf_op jit(solution)/shard_map/gather | solution.py:131
  21.9 2.7 %gather_fusion = bf16[56,128,256]{2,1,0:T(8,128)(2,1)} fusion(bf16[28,128,256]{2,1,0:T(8,128)(2,1)S(1)} %constant_dynamic-update-slice_fusion, s32[1024]{0:T(1024)S(1)} %pad_clamp_fusion.1), kind=kCustom, calls=%fused_computation | custom fusion | bytes 7340256 | tf_op jit(solution)/shard_map/gather | solution.py:131
  24.7 3.5 %fusion.8 = (f32[14,128]{1,0:T(8,128)S(1)}, f32[14,128,4,128]{1,3,2,0:T(8,128)S(1)}) fusion(pred[14,4]{1,0:T(8,128)(4,1)S(1)} %iota_compare_fusion, bf16[14,4,128,256]{3,2,1,0:T(8,128)(2,1)} %bitcast.88, bf16[14,128,256]{2,1,0:T(8,128)(2,1)S(1)} %copy-done.5, bf16[14,128,256]{2,1,0:T(8,128)(2,1)} %param.16), kind=kOutput, calls=%fused_computation.23 | convolution fusion | flops 474347776 | bytes 9182264 | tf_op jit(solution)/shard_map/bpc,blkc->bplk/dot_general | solution.py:91
  28.2 0.8 fusion.11
  29.0 1.2 %copy-done.3 = bf16[56,128,256]{2,1,0:T(8,128)(2,1)S(1)} copy-done((bf16[56,128,256]{2,1,0:T(8,128)(2,1)S(1)}, bf16[56,128,256]{2,1,0:T(8,128)(2,1)}, u32[]{:S(2)}) %copy-start.3) | copy-done | bytes 3670040
  30.2 1.2 %bitcast_convert_fusion.1 = bf16[14,128,256]{2,1,0:T(8,128)(2,1)S(1)} fusion(bf16[14,4,128,256]{3,2,1,0:T(8,128)(2,1)S(1)} %bitcast.89, f32[14,128,4,128]{1,3,2,0:T(8,128)S(1)} %get-tuple-element.57, f32[14,128]{1,0:T(8,128)S(1)} %fusion.11, f32[14,128]{1,0:T(8,128)S(1)} %get-tuple-element.56, pred[14,4]{1,0:T(8,128)(4,1)S(1)} %iota_compare_fusion), kind=kOutput, calls=%fused_computation.69 | convolution fusion | flops 474808320 | bytes 8271928 | tf_op jit(solution)/shard_map/bplk,blkc->bpc/dot_general | solution.py:99
  31.4 0.0 copy-start.12
  31.4 2.7 %multiply_reduce_fusion.3 = (f32[14,128]{1,0:T(8,128)S(1)}, f32[14,128]{1,0:T(8,128)S(1)}) fusion(f32[14,4,128]{2,1,0:T(4,128)S(1)} %get-tuple-element.55, f32[14,128]{1,0:T(8,128)S(1)} %fusion.11, f32[14,128]{1,0:T(8,128)S(1)} %get-tuple-element.56, f32[14,128,4,128]{1,3,2,0:T(8,128)S(1)} %get-tuple-element.57, pred[14,4]{1,0:T(8,128)(4,1)S(1)} %iota_compare_fusion, ...), kind=kLoop, calls=%fused_computation.20 | loop fusion | flops 7336448 | bytes 3756088 | tf_op jit(solution)/shard_map/reduce_sum | solution.py:79
  34.2 0.0 copy-start.11
  34.2 1.3 %add_add_fusion.1 = f32[1792,768]{1,0:T(8,128)S(1)} fusion(bf16[1792,256]{1,0:T(8,128)(2,1)S(1)} %bitcast.95, bf16[256,768]{1,0:T(8,128)(2,1)S(1)} %copy-done, f32[768]{0:T(1024)S(1)} %copy-done.12, f32[768]{0:T(1024)S(1)} %get-tuple-element.36, f32[1792]{0:T(1024)S(1)} %subtract_bitcast_fusion.2, f32[768]{0:T(1024)S(1)} %get-tuple-element.35, ...), kind=kOutput, calls=%fused_computation.4 | convolution fusion | flops 711524352 | bytes 6839296 | tf_op jit(solution)/shard_map/dot_general | solution.py:48
  35.4 0.8 copy-done.8
  36.2 1.4 %fusion.16 = f32[1792,256]{1,0:T(8,128)S(1)} fusion(bf16[256,256]{1,0:T(8,128)(2,1)S(1)} %copy-done.11, bf16[1792,256]{1,0:T(8,128)(2,1)S(1)} %bitcast.92, f32[1792,768]{1,0:T(8,128)S(1)} %add_add_fusion.1, f32[1792,512]{1,0:T(8,128)S(1)} %copy-done.8), kind=kOutput, calls=%fused_computation.33 | convolution fusion | flops 242679808 | bytes 12976128 | tf_op jit(solution)/shard_map/dot_general | solution.py:58
  37.6 0.2 fusion.21
  37.8 1.8 %copy-done.2 = bf16[56,128,256]{2,1,0:T(8,128)(2,1)S(1)} copy-done((bf16[56,128,256]{2,1,0:T(8,128)(2,1)S(1)}, bf16[56,128,256]{2,1,0:T(8,128)(2,1)}, u32[]{:S(2)}) %copy-start.2) | copy-done | bytes 3670040
  39.6 1.1 %fusion.9 = (f32[14,128]{1,0:T(8,128)S(1)}, f32[14,128,4,128]{1,3,2,0:T(8,128)S(1)}) fusion(pred[14,4]{1,0:T(8,128)(4,1)S(1)} %iota_compare_fusion, bf16[14,4,128,256]{3,2,1,0:T(8,128)(2,1)S(1)} %bitcast.84, bf16[14,128,256]{2,1,0:T(8,128)(2,1)S(1)} %fusion.21), kind=kOutput, calls=%fused_computation.24 | convolution fusion | flops 472512768 | bytes 8264760 | tf_op jit(solution)/shard_map/bpc,blkc->bplk/dot_general | solution.py:91
  40.8 0.0 copy-start.10
  40.8 0.9 fusion.13
  41.7 0.3 copy-done.10
  41.9 4.0 %fusion.4 = (f32[14,128]{1,0:T(8,128)S(1)}, f32[14,128]{1,0:T(8,128)S(1)}, f32[14,128]{1,0:T(8,128)S(1)}, f32[14,4,128,128]{3,2,1,0:T(8,128)S(1)}) fusion(f32[14,128]{1,0:T(8,128)S(1)} %fusion.13, f32[14,128]{1,0:T(8,128)S(1)} %get-tuple-element.58, f32[14,128,4,128]{1,3,2,0:T(8,128)S(1)} %get-tuple-element.59, pred[14,4]{1,0:T(8,128)(4,1)S(1)} %iota_compare_fusion, ...), kind=kOutput, calls=%fused_computation.11 | convolution fusion | flops 478931712 | bytes 12020792 | tf_op jit(solution)/shard_map/bpc,blkc->bplk/dot_general | solution.py:148
  46.0 1.7 %fusion.7 = (bf16[14,128,4,128]{1,3,2,0:T(8,128)(2,1)S(1)}, bf16[14,128,4,128]{1,3,2,0:T(8,128)(2,1)S(1)}) fusion(f32[14,4,128,128]{3,2,1,0:T(8,128)S(1)} %get-tuple-element.60, f32[14,128]{1,0:T(8,128)S(1)} %get-tuple-element.30, f32[14,128]{1,0:T(8,128)S(1)} %fusion.13, f32[14,128]{1,0:T(8,128)S(1)} %get-tuple-element.58, ...), kind=kLoop, calls=%fused_computation.14 | loop fusion | flops 8257536 | bytes 11031608 | tf_op jit(solution)/shard_map/convert_element_type | solution.py:152
  47.7 0.9 bitcast_convert_fusion
  48.6 3.6 %fusion = f32[14,4,128,256]{3,2,1,0:T(8,128)} fusion(bf16[14,128,4,128]{1,3,2,0:T(8,128)(2,1)S(1)} %get-tuple-element.37, bf16[14,128,4,128]{1,3,2,0:T(8,128)(2,1)S(1)} %get-tuple-element.38, bf16[14,128,256]{2,1,0:T(8,128)(2,1)S(1)} %fusion.21, bf16[14,128,256]{2,1,0:T(8,128)(2,1)S(1)} %copy-done.10), kind=kOutput, calls=%fused_computation.5 | convolution fusion | flops 950534144 | bytes 12845056 | tf_op jit(solution)/shard_map/bplk,bpc->blkc/dot_general | solution.py:155
  52.2 2.3 %broadcast_in_dim.26 = f32[28,128,256]{2,1,0:T(8,128)} broadcast(f32[]{:T(128)} %constant.172.clone.1), dimensions={} | broadcast | bytes 3670020 | tf_op jit(solution)/shard_map/broadcast_in_dim | solution.py:157
  54.6 18.8 %scatter_fusion = f32[28,128,256]{2,1,0:T(8,128)} fusion(f32[28,128,256]{2,1,0:T(8,128)} %broadcast_in_dim.26, s32[56]{0:T(128)S(1)} %fusion.68, f32[56,128,256]{2,1,0:T(8,128)} %bitcast.87), kind=kCustom, calls=%fused_computation.2 | custom fusion | flops 1835008 | bytes 22020320 | tf_op jit(solution)/shard_map/scatter-add | solution.py:158
  73.3 1.8 %slice.143 = f32[14,128,256]{2,1,0:T(8,128)S(1)} slice(f32[28,128,256]{2,1,0:T(8,128)} %scatter_fusion), slice={[7:21], [0:128], [0:256]} | slice | bytes 3670016 | tf_op jit(solution)/shard_map/slice | solution.py:163
  75.1 0.8 copy-done.1
  75.9 0.1 fusion.75
  76.1 0.6 copy.33
  76.7 1.9 %collective-permute-start.2 = (f32[7,128,256]{2,1,0:T(8,128)S(1)}, f32[7,128,256]{2,1,0:T(8,128)S(1)}, u32[]{:S(2)}, u32[]{:S(2)}) collective-permute-start(f32[7,128,256]{2,1,0:T(8,128)S(1)} %get-tuple-element.40), channel_id=1, source_target_pairs={{1,0},{2,1},{3,2},{4,3},{5,4},{6,5},{7,6},{8,7},{9,8},{10,9},{11,1... | collective-permute-start | bytes 2752520 | tf_op jit(solution)/shard_map/ppermute | solution.py:30
  78.6 4.0 %collective-permute-start.3 = (f32[7,128,256]{2,1,0:T(8,128)S(1)}, f32[7,128,256]{2,1,0:T(8,128)S(1)}, u32[]{:S(2)}, u32[]{:S(2)}) collective-permute-start(f32[7,128,256]{2,1,0:T(8,128)S(1)} %get-tuple-element.39), channel_id=1, source_target_pairs={{0,1},{1,2},{2,3},{3,4},{4,5},{5,6},{6,7},{7,8},{8,9},{9,10},{10,1... | collective-permute-start | bytes 2752520 | tf_op jit(solution)/shard_map/ppermute | solution.py:30
  82.7 0.0 copy-start.9
  82.7 1.3 %add_add_fusion = f32[1792,768]{1,0:T(8,128)S(1)} fusion(bf16[1792,256]{1,0:T(8,128)(2,1)S(1)} %bitcast.93, bf16[256,768]{1,0:T(8,128)(2,1)S(1)} %copy-done, f32[1792]{0:T(1024)S(1)} %subtract_bitcast_fusion, f32[1792]{0:T(1024)S(1)} %subtract_bitcast_fusion.1, f32[768]{0:T(1024)S(1)} %copy-done.12, f32[768]{0:T(1024)S(1)} %get-tuple-element.36, ...), kind=kOutput, calls=%fused_computation.3 | convolution fusion | flops 711524352 | bytes 6839296 | tf_op jit(solution)/shard_map/dot_general | solution.py:48
  84.0 0.6 fusion.58
  84.6 2.6 %fusion.19 = f32[1792,256]{1,0:T(8,128)} fusion(bf16[256,256]{1,0:T(8,128)(2,1)S(1)} %copy-done.11, f32[1792,768]{1,0:T(8,128)S(1)} %add_add_fusion, f32[1792,256]{1,0:T(8,128)S(1)} %fusion.16, f32[1792,512]{1,0:T(8,128)S(1)} %fusion.58), kind=kOutput, calls=%fused_computation.36 | convolution fusion | flops 241762304 | bytes 14811136 | tf_op jit(solution)/shard_map/dot_general | solution.py:58
  87.2 4.4 %collective-permute-done.2 = f32[7,128,256]{2,1,0:T(8,128)S(1)} collective-permute-done((f32[7,128,256]{2,1,0:T(8,128)S(1)}, f32[7,128,256]{2,1,0:T(8,128)S(1)}, u32[]{:S(2)}, u32[]{:S(2)}) %collective-permute-start.2) | collective-permute-done | bytes 917536 | tf_op jit(solution)/shard_map/ppermute | solution.py:30
  91.6 0.1 fusion.53
  91.7 10.1 %collective-permute-done.3 = f32[7,128,256]{2,1,0:T(8,128)S(1)} collective-permute-done((f32[7,128,256]{2,1,0:T(8,128)S(1)}, f32[7,128,256]{2,1,0:T(8,128)S(1)}, u32[]{:S(2)}, u32[]{:S(2)}) %collective-permute-start.3) | collective-permute-done | bytes 917536 | tf_op jit(solution)/shard_map/ppermute | solution.py:30
  101.9 0.2 fusion.52
  102.1 0.0 copy-start.4
  102.1 1.2 %copy-done.4 = f32[14,128,256]{2,1,0:T(8,128)} copy-done((f32[14,128,256]{2,1,0:T(8,128)}, f32[14,128,256]{2,1,0:T(8,128)S(1)}, u32[]{:S(2)}) %copy-start.4) | copy-done | bytes 1835032
  (29 shorter events, 0.1 us)
Async XLA Ops:
  0.6 33.5 %copy-start = (bf16[256,768]{1,0:T(8,128)(2,1)S(1)}, bf16[256,768]{1,0:T(8,128)(2,1)}, u32[]{:S(2)}) copy-start(bf16[256,768]{1,0:T(8,128)(2,1)} %param.24) | copy-start | bytes 1179652
  0.6 17.5 %copy-start.7 = (bf16[14,128,256]{2,1,0:T(8,128)(2,1)S(1)}, bf16[14,128,256]{2,1,0:T(8,128)(2,1)}, u32[]{:S(2)}) copy-start(bf16[14,128,256]{2,1,0:T(8,128)(2,1)} %param.17) | copy-start | bytes 2752516
  2.7 14.3 %collective-permute-start = (bf16[7,128,256]{2,1,0:T(8,128)(2,1)S(1)}, bf16[7,128,256]{2,1,0:T(8,128)(2,1)}, u32[]{:S(2)}, u32[]{:S(2)}) collective-permute-start(bf16[7,128,256]{2,1,0:T(8,128)(2,1)S(1)} %get-tuple-element.42), channel_id=1, source_target_pairs={{0,1},{1,2},{2,3},{3,4},{4,5},{5,6},{6,7},{7,8},{8,9},{9,10},{10,1... | collective-permute-start | bytes 1376264 | tf_op jit(solution)/shard_map/ppermute | solution.py:21
  7.3 10.9 %collective-permute-start.1 = (bf16[7,128,256]{2,1,0:T(8,128)(2,1)}, bf16[7,128,256]{2,1,0:T(8,128)(2,1)}, u32[]{:S(2)}, u32[]{:S(2)}) collective-permute-start(bf16[7,128,256]{2,1,0:T(8,128)(2,1)} %get-tuple-element.41), channel_id=1, source_target_pairs={{1,0},{2,1},{3,2},{4,3},{5,4},{6,5},{7,6},{8,7},{9,8},{10,9},{11,1... | collective-permute-start | bytes 1376264 | tf_op jit(solution)/shard_map/ppermute | solution.py:22
  21.9 2.7 %copy-start.5 = (bf16[14,128,256]{2,1,0:T(8,128)(2,1)S(1)}, bf16[14,128,256]{2,1,0:T(8,128)(2,1)}, u32[]{:S(2)}) copy-start(bf16[14,128,256]{2,1,0:T(8,128)(2,1)} %param.18) | copy-start | bytes 2752516
  28.1 2.0 %copy-start.3 = (bf16[56,128,256]{2,1,0:T(8,128)(2,1)S(1)}, bf16[56,128,256]{2,1,0:T(8,128)(2,1)}, u32[]{:S(2)}) copy-start(bf16[56,128,256]{2,1,0:T(8,128)(2,1)} %gather_fusion) | copy-start | bytes 11010052
  31.4 2.8 %copy-start.12 = (f32[768]{0:T(1024)S(1)}, f32[768]{0:T(1024)}, u32[]{:S(2)}) copy-start(f32[768]{0:T(1024)} %param.27) | copy-start | bytes 9220
  34.2 2.0 %copy-start.8 = (f32[1792,512]{1,0:T(8,128)S(1)}, f32[1792,512]{1,0:T(8,128)}, u32[]{:S(2)}) copy-start(f32[1792,512]{1,0:T(8,128)} %fusion.77) | copy-start | bytes 11010052
  34.2 2.0 %copy-start.11 = (bf16[256,256]{1,0:T(8,128)(2,1)S(1)}, bf16[256,256]{1,0:T(8,128)(2,1)}, u32[]{:S(2)}) copy-start(bf16[256,256]{1,0:T(8,128)(2,1)} %param.25) | copy-start | bytes 393220
  36.2 1.4 %copy-start.6 = (bf16[14,128,256]{2,1,0:T(8,128)(2,1)S(1)}, bf16[14,128,256]{2,1,0:T(8,128)(2,1)}, u32[]{:S(2)}) copy-start(bf16[14,128,256]{2,1,0:T(8,128)(2,1)} %param.16) | copy-start | bytes 2752516
  37.6 2.0 %copy-start.2 = (bf16[56,128,256]{2,1,0:T(8,128)(2,1)S(1)}, bf16[56,128,256]{2,1,0:T(8,128)(2,1)}, u32[]{:S(2)}) copy-start(bf16[56,128,256]{2,1,0:T(8,128)(2,1)} %gather_fusion.1) | copy-start | bytes 11010052
  40.8 1.2 %copy-start.10 = (bf16[14,128,256]{2,1,0:T(8,128)(2,1)S(1)}, bf16[14,128,256]{2,1,0:T(8,128)(2,1)}, u32[]{:S(2)}) copy-start(bf16[14,128,256]{2,1,0:T(8,128)(2,1)} %param.19) | copy-start | bytes 2752516
  73.3 2.6 %copy-start.1 = (f32[28,128,256]{2,1,0:T(8,128)S(1)}, f32[28,128,256]{2,1,0:T(8,128)}, u32[]{:S(2)}) copy-start(f32[28,128,256]{2,1,0:T(8,128)} %scatter_fusion) | copy-start | bytes 11010052
  76.7 14.9 %collective-permute-start.2 = (f32[7,128,256]{2,1,0:T(8,128)S(1)}, f32[7,128,256]{2,1,0:T(8,128)S(1)}, u32[]{:S(2)}, u32[]{:S(2)}) collective-permute-start(f32[7,128,256]{2,1,0:T(8,128)S(1)} %get-tuple-element.40), channel_id=1, source_target_pairs={{1,0},{2,1},{3,2},{4,3},{5,4},{6,5},{7,6},{8,7},{9,8},{10,9},{11,1... | collective-permute-start | bytes 2752520 | tf_op jit(solution)/shard_map/ppermute | solution.py:30
  78.6 23.2 %collective-permute-start.3 = (f32[7,128,256]{2,1,0:T(8,128)S(1)}, f32[7,128,256]{2,1,0:T(8,128)S(1)}, u32[]{:S(2)}, u32[]{:S(2)}) collective-permute-start(f32[7,128,256]{2,1,0:T(8,128)S(1)} %get-tuple-element.39), channel_id=1, source_target_pairs={{0,1},{1,2},{2,3},{3,4},{4,5},{5,6},{6,7},{7,8},{8,9},{9,10},{10,1... | collective-permute-start | bytes 2752520 | tf_op jit(solution)/shard_map/ppermute | solution.py:30
  82.7 1.3 %copy-start.9 = (bf16[256,512]{1,0:T(8,128)(2,1)S(1)}, bf16[256,512]{1,0:T(8,128)(2,1)}, u32[]{:S(2)}) copy-start(bf16[256,512]{1,0:T(8,128)(2,1)} %param.23) | copy-start | bytes 786436
  102.1 1.2 %copy-start.4 = (f32[14,128,256]{2,1,0:T(8,128)}, f32[14,128,256]{2,1,0:T(8,128)S(1)}, u32[]{:S(2)}) copy-start(f32[14,128,256]{2,1,0:T(8,128)S(1)} %fusion.52) | copy-start | bytes 5505028
where the time goes:
time: 104 us; the launch traced here: 103 us
  other arithmetic  27.2 us (26%)
  matrix products  25 us (24%)
  local copies, waits for them, and re-layouts  23.1 us (22%)
  waiting for transfers between devices  14.5 us (14%)
  starting transfers between devices  12.4 us (12%)
  between operations  1.05 us (1%)
    scatter-add x1, other arithmetic, local(): summed.at[local_ids.reshape(-1)]  18.8 us
    ppermute x2, waiting for transfers between devices, passed_along(): return lax.ppermute(block, axis, route)  14.5 us
    unnamed x29, local copies, waits for them, and re-layouts  7.81 us
    ppermute x2, starting transfers between devices, passed_along(): return lax.ppermute(block, axis, route)  5.95 us
    gather x2, local copies, waits for them, and re-layouts, local(): key_blocks = window[local_ids]  5.41 us
    dot_general x2, matrix products, attend(): jnp.einsum('bpc,blkc->bplk', queries, key_blocks, preferred_element_type=...  4.59 us
    ppermute x1, starting transfers between devices, with_halo(): before = lax.ppermute(last, axis, up)  4.5 us
    dot_general x2, matrix products, motion_update(): jnp.dot(hidden.astype(jnp.bfloat16), hid_weight, preferred_element_type=j...  4.3 us
  transfers between devices with their start and end apart: 4, of which 2 were waited for; matrix products, arithmetic and copies ran while one was open for 13% of the time, Pallas kernels for 0%

commit v1 on v0

v1 whole, which is shorter than its diff:
```python
import functools
import math

import jax
import jax.numpy as jnp
from jax import lax
from jax.experimental import pallas as pl
from jax.experimental.pallas import tpu as pltpu
from jax.sharding import PartitionSpec as P

PH = 8
PW = 16
BW = 7
ITERS = 2
GROUP = 2
F32 = jnp.float32
BF16 = jnp.bfloat16


def dot_nt(a, b):
    return lax.dot_general(a, b, (((1,), (1,)), ((), ())), preferred_element_type=F32)


def dot_tn(a, b):
    return lax.dot_general(a, b, (((0,), (0,)), ((), ())), preferred_element_type=F32)


def sigmoid(x):
    return 0.5 * jnp.tanh(0.5 * x) + 0.5


def gates(h, motion, flow_r, flow_c, hid_w, in_w, cand_w, disp, bias):
    ch = h.shape[1]
    g = jnp.dot(h.astype(BF16), hid_w, preferred_element_type=F32)
    e = jnp.dot(motion, in_w, preferred_element_type=F32)
    e = e + (flow_r * disp[0:1] + (flow_c * disp[1:2] + bias))
    z = sigmoid(g[:, :ch] + e[:, :ch])
    r = sigmoid(g[:, ch:] + e[:, ch : 2 * ch])
    c = jnp.tanh(
        jnp.dot((r * h).astype(BF16), cand_w, preferred_element_type=F32) + e[:, 2 * ch :]
    )
    return h + z * (c - h)


def slot_places(search, offs, refine, b, slots, base):
    return [search[b, l] + offs[refine, b] - base for l in range(slots)]


def attention(q, keys, places, length, row_at, col_at):
    slots = len(places)
    cells = q.shape[0]
    scale = 1.0 / math.sqrt(q.shape[1])
    s = dot_nt(q, keys) * scale
    parts = [s[:, l * cells : (l + 1) * cells] for l in range(slots)]
    for l in range(1, slots):
        parts[l] = parts[l] + jnp.where(l < length, 0.0, -1e30).astype(F32)
    top = functools.reduce(jnp.maximum, parts)
    m = jnp.max(top, axis=1, keepdims=True)
    exps = [jnp.exp(p - m) for p in parts]
    total = jnp.sum(functools.reduce(jnp.add, exps), axis=1, keepdims=True)
    inv = 1.0 / total
    w = [x * inv for x in exps]
    half = [x.astype(BF16) for x in w]
    motion = jnp.dot(jnp.concatenate(half, axis=1), keys, preferred_element_type=F32)
    k = lax.broadcasted_iota(jnp.int32, (1, cells), 1)
    ky = (k // PW).astype(F32) / PH
    kx = (k % PW).astype(F32) / PW
    fr = fc = None
    for l in range(slots):
        row = (places[l] * 9363) >> 16
        col = places[l] - row * BW
        y = w[l] * (ky + (row - row_at).astype(F32))
        x = w[l] * (kx + (col - col_at).astype(F32))
        fr, fc = (y, x) if l == 0 else (fr + y, fc + x)
    p = lax.broadcasted_iota(jnp.int32, (cells, 1), 0)
    fr = jnp.sum(fr, axis=1, keepdims=True) - (p // PW).astype(F32) / PH
    fc = jnp.sum(fc, axis=1, keepdims=True) - (p % PW).astype(F32) / PW
    return w, half, motion.astype(BF16), fr, fc


def main_kernel(
    search, offs, lens, first_h, before_h, second_h, after_h, hidden_h, cot_h,
    hid_w, in_w, cand_w, disp, bias,
    h_out, mot_out, fcol_out, flow_out, own_out, low_out, up_out,
    win, first, hid0, cot, acc, sems,
):
    blocks, cells, ch = first_h.shape
    slots = search.shape[1]
    copies = [
        pltpu.make_async_copy(second_h, win.at[pl.ds(BW, blocks)], sems.at[0]),
        pltpu.make_async_copy(before_h, win.at[pl.ds(0, BW)], sems.at[1]),
        pltpu.make_async_copy(after_h, win.at[pl.ds(BW + blocks, BW)], sems.at[2]),
        pltpu.make_async_copy(first_h, first, sems.at[3]),
        pltpu.make_async_copy(hidden_h, hid0, sems.at[4]),
        pltpu.make_async_copy(cot_h, cot, sems.at[5]),
    ]
    for c in copies:
        c.start()
    base = lax.axis_index("tile") * blocks - BW
    acc[...] = jnp.zeros_like(acc)
    for c in copies:
        c.wait()

    def body(step, carry):
        bs = [step * GROUP + j for j in range(GROUP)]
        at = [slot_row_col(b) for b in bs]
        h = [hid0[b].astype(F32) for b in bs]
        for refine in range(ITERS):
            outs = []
            for j, b in enumerate(bs):
                places = slot_places(search, offs, refine, b, slots, base)
                keys = jnp.concatenate([win[i] for i in places], axis=0)
                q = (first[b].astype(F32) + h[j]).astype(BF16)
                w, half, motion, fr, fc = attention(q, keys, places, lens[b], *at[j])
                outs.append((motion, fr, fc))
                if refine == ITERS - 1:
                    ct = cot[b]
                    dw = dot_nt(ct, keys)
                    dws = [dw[:, l * cells : (l + 1) * cells] for l in range(slots)]
                    prod = functools.reduce(jnp.add, [w[l] * dws[l] for l in range(slots)])
                    delta = jnp.sum(prod, axis=1, keepdims=True)
                    ds = [
                        (w[l] * (dws[l] - delta) * (1.0 / math.sqrt(ch))).astype(BF16)
                        for l in range(slots)
                    ]
                    stacked = jnp.concatenate(
                        [jnp.concatenate(half, axis=1), jnp.concatenate(ds, axis=1)], axis=0
                    )
                    contrib = dot_tn(stacked, jnp.concatenate([ct, q], axis=0))
                    for l in range(slots):
                        acc[places[l]] += contrib[l * cells : (l + 1) * cells]
            motion, fr, fc = (jnp.concatenate(t, axis=0) for t in zip(*outs))
            if refine < ITERS - 1:
                hcat = jnp.concatenate(h, axis=0)
                hcat = gates(
                    hcat, motion, fr, fc, hid_w[...], in_w[...], cand_w[...], disp[...], bias[...]
                )
                h = [hcat[j * cells : (j + 1) * cells] for j in range(GROUP)]
            else:
                lane = lax.broadcasted_iota(jnp.int32, (cells, cells), 1)
                for j, b in enumerate(bs):
                    mot_out[b] = outs[j][0]
                    h_out[b] = h[j]
                    both = jnp.where(lane == 0, outs[j][1], outs[j][2])
                    fcol_out[b] = both
                    flow_out[b] = both.T[0:2]
        return carry

    lax.fori_loop(0, blocks // GROUP, body, 0)
    own_out[...] = acc[BW : BW + blocks]
    low_out[...] = acc[0:BW].astype(BF16)
    up_out[...] = acc[BW + blocks :].astype(BF16)


def slot_row_col(b):
    row = (b * 9363) >> 16
    return row + 1, b - row * BW


def last_gates_kernel(h, mot, fcol, hid_w, in_w, cand_w, disp, bias, out):
    g, cells, ch = h.shape
    f = fcol[...].reshape(g * cells, cells)
    res = gates(
        h[...].reshape(g * cells, ch),
        mot[...].reshape(g * cells, ch),
        f[:, 0:1],
        f[:, 1:2],
        hid_w[...], in_w[...], cand_w[...], disp[...], bias[...],
    )
    out[...] = res.reshape(g, cells, ch)


def local(
    first_feat, second_feat, hidden_init, cotangent, search_list, offsets, lengths,
    hid_weight, in_weight, cand_weight, disp_weight, gate_bias,
):
    blocks, cells, ch = first_feat.shape
    n = lax.axis_size("tile")
    up = [(i, i + 1) for i in range(n - 1)]
    down = [(i + 1, i) for i in range(n - 1)]
    before = lax.ppermute(second_feat[blocks - BW :], "tile", up)
    after = lax.ppermute(second_feat[:BW], "tile", down)
    bias = gate_bias.reshape(1, -1)
    smem = pl.BlockSpec(memory_space=pltpu.SMEM)
    hbm = pl.BlockSpec(memory_space=pl.ANY)
    vmem = pl.BlockSpec(memory_space=pltpu.VMEM)
    sds = jax.ShapeDtypeStruct
    macs = blocks * cells * (4 * cells * ch * 7 + ch * ch * 6)
    h1, mot, fcol, flow, own, low, high = pl.pallas_call(
        main_kernel,
        out_shape=[
            sds((blocks, cells, ch), F32),
            sds((blocks, cells, ch), BF16),
            sds((blocks, cells, cells), F32),
            sds((blocks, 2, cells), F32),
            sds((blocks, cells, ch), F32),
            sds((BW, cells, ch), BF16),
            sds((BW, cells, ch), BF16),
        ],
        in_specs=[smem] * 3 + [hbm] * 6 + [vmem] * 5,
        out_specs=[vmem] * 7,
        scratch_shapes=[
            pltpu.VMEM((blocks + 2 * BW, cells, ch), BF16),
            pltpu.VMEM((blocks, cells, ch), BF16),
            pltpu.VMEM((blocks, cells, ch), BF16),
            pltpu.VMEM((blocks, cells, ch), BF16),
            pltpu.VMEM((blocks + 2 * BW, cells, ch), F32),
            pltpu.SemaphoreType.DMA((6,)),
        ],
        compiler_params=pltpu.CompilerParams(vmem_limit_bytes=48 * 2**20),
        cost_estimate=pl.CostEstimate(flops=2 * macs, bytes_accessed=10 * 2**20, transcendentals=0),
    )(
        search_list, offsets, lengths, first_feat, before, second_feat, after,
        hidden_init, cotangent, hid_weight, in_weight, cand_weight, disp_weight, bias,
    )
    from_next = lax.ppermute(low, "tile", down)
    from_prev = lax.ppermute(high, "tile", up)
    step = lambda i: (i, 0, 0)
    whole = lambda i: (0, 0)
    hidden = pl.pallas_call(
        last_gates_kernel,
        out_shape=sds((blocks, cells, ch), F32),
        grid=(blocks // GROUP,),
        in_specs=[
            pl.BlockSpec((GROUP, cells, ch), step),
            pl.BlockSpec((GROUP, cells, ch), step),
            pl.BlockSpec((GROUP, cells, cells), step),
            pl.BlockSpec(hid_weight.shape, whole),
            pl.BlockSpec(in_weight.shape, whole),
            pl.BlockSpec(cand_weight.shape, whole),
            pl.BlockSpec(disp_weight.shape, whole),
            pl.BlockSpec(bias.shape, whole),
        ],
        out_specs=pl.BlockSpec((GROUP, cells, ch), step),
        compiler_params=pltpu.CompilerParams(vmem_limit_bytes=24 * 2**20),
        cost_estimate=pl.CostEstimate(
            flops=2 * blocks * cells * ch * ch * 6, bytes_accessed=5 * 2**20, transcendentals=0
        ),
    )(h1, mot, fcol, hid_weight, in_weight, cand_weight, disp_weight, bias)
    own = jnp.concatenate(
        [own[:BW] + from_prev.astype(F32), own[BW:-BW], own[-BW:] + from_next.astype(F32)], axis=0
    ) if blocks > 2 * BW else jnp.concatenate(
        [own[:BW] + from_prev.astype(F32), own[BW:] + from_next.astype(F32)], axis=0
    )
    return hidden, flow, own


def solution(mesh):
    lead = ("grp", "tile")
    return jax.shard_map(
        local,
        mesh=mesh,
        in_specs=(
            P(lead, None, None), P(lead, None, None), P(lead, None, None), P(lead, None, None),
            P(lead, None), P(None, lead), P(lead), P(), P(), P(), P(), P(),
        ),
        out_specs=(P(lead, None, None), P(lead, None, None), P(lead, None, None)),
        check_vma=False,
    )
```

time: 104 us -> 59.6 us (0.57)
  Pallas kernels: 0 us -> 29.1 us
  other arithmetic: 27.2 us -> 1.56 us
  matrix products: 25 us -> 0 us
  local copies, waits for them, and re-layouts: 23.1 us -> 3.75 us
  waiting for transfers between devices: 14.5 us -> 11.4 us
    pallas_call x0 -> x2, Pallas kernels: none -> 29.1 us  [the longest x1 24.2 us: local(): pl.pallas_call(main_kernel, out_shape=[sds((blocks, cells, ch), F32), sds...]
    dot_general x12 -> x0, matrix products: 25 us -> none  [the longest x2 4.59 us: attend(): jnp.einsum('bpc,blkc->bplk', queries, key_blocks, preferred_element_type=...]
    scatter-add x3 -> x0, other arithmetic: 19.1 us -> none  [the longest x1 18.8 us: local(): summed.at[local_ids.reshape(-1)]]
    unnamed x29 -> x23, local copies, waits for them, and re-layouts: 7.81 us -> 1.63 us
    gather x2 -> x0, local copies, waits for them, and re-layouts: 5.41 us -> none  [local(): key_blocks = window[local_ids]]
    reduce_sum x3 -> x0, other arithmetic: 4.46 us -> none  [the longest x1 2.73 us: displacement(): jnp.sum(weights * key_y[:, None], axis=(2, 3))]
    ppermute x4, waiting for transfers between devices: 14.5 us -> 11.4 us  [the longest x1 5.08 us: local(): before = lax.ppermute(second_feat[blocks - BW:], 'tile', up)]
    slice x4 -> x1, local copies, waits for them, and re-layouts: 4.8 us -> 2.12 us  [local(): after = lax.ppermute(second_feat[:BW], 'tile', down)]
  transfers between devices with their start and end apart: 4 -> 4, of which waited for: 2 -> 3; matrix products, arithmetic and copies ran while one was open for 13% -> 0% of each run, Pallas kernels for 0% -> 8%
where the time goes in v1:
time: 59.6 us; the launch traced here: 59.4 us
  Pallas kernels  29.1 us (49%)
  starting transfers between devices  12.7 us (21%)
  waiting for transfers between devices  11.4 us (19%)
  local copies, waits for them, and re-layouts  3.75 us (6%)
  other arithmetic  1.56 us (3%)
  between operations  0.81 us (1%)
    pallas_call x1, Pallas kernels, local(): pl.pallas_call(main_kernel, out_shape=[sds((blocks, cells, ch), F32), sds...  24.2 us
    ppermute x1, waiting for transfers between devices, local(): before = lax.ppermute(second_feat[blocks - BW:], 'tile', up)  5.08 us
    pallas_call x1, Pallas kernels, local(): pl.pallas_call(last_gates_kernel, out_shape=sds((blocks, cells, ch), F32)...  4.9 us
    ppermute x1, starting transfers between devices, local(): before = lax.ppermute(second_feat[blocks - BW:], 'tile', up)  4.46 us
    ppermute x1, starting transfers between devices, local(): from_prev = lax.ppermute(high, 'tile', up)  4.4 us
    ppermute x1, waiting for transfers between devices, local(): after = lax.ppermute(second_feat[:BW], 'tile', down)  4.3 us
    slice x1, local copies, waits for them, and re-layouts, local(): after = lax.ppermute(second_feat[:BW], 'tile', down)  2.12 us
    ppermute x1, waiting for transfers between devices, local(): from_prev = lax.ppermute(high, 'tile', up)  1.99 us
  transfers between devices with their start and end apart: 4, of which 3 were waited for; matrix products, arithmetic and copies ran while one was open for 0% of the time, Pallas kernels for 8%

profile of v1, /device:TPU:1, one launch (start us, length us, event | category | flops | bytes accessed | tf_op | source)
XLA Modules:
  0.0 59.4 jit_solution(7566076902415528920)
XLA Ops:
  0.6 0.0 copy-start.9
  0.6 0.0 copy-start.10
  0.7 0.0 copy-start.4
  0.7 0.0 copy-start.3
  0.7 0.0 copy-start.1
  0.7 0.0 copy-start.2
  0.7 0.0 copy-start.7
  0.7 0.0 copy-start.6
  0.7 0.0 copy-start.5
  0.7 2.1 %fusion = (bf16[7,128,256]{2,1,0:T(8,128)(2,1)}, bf16[7,128,256]{2,1,0:T(8,128)(2,1)S(1)}) fusion(bf16[14,128,256]{2,1,0:T(8,128)(2,1)} %second_h.1), kind=kLoop, calls=%fused_computation.3 | loop fusion | bytes 1835008 | tf_op jit(solution)/shard_map/slice | solution.py:182
  2.8 2.0 %collective-permute-start.1 = (bf16[7,128,256]{2,1,0:T(8,128)(2,1)}, bf16[7,128,256]{2,1,0:T(8,128)(2,1)S(1)}, u32[]{:S(2)}, u32[]{:S(2)}) collective-permute-start(bf16[7,128,256]{2,1,0:T(8,128)(2,1)} %get-tuple-element.19), channel_id=1, source_target_pairs={{1,0},{2,1},{3,2},{4,3},{5,4},{6,5},{7,6},{8,7},{9,8},{10,9},{11,1... | collective-permute-start | bytes 1376264 | tf_op jit(solution)/shard_map/ppermute | solution.py:182
  4.8 4.5 %collective-permute-start = (bf16[7,128,256]{2,1,0:T(8,128)(2,1)S(1)}, bf16[7,128,256]{2,1,0:T(8,128)(2,1)S(1)}, u32[]{:S(2)}, u32[]{:S(2)}) collective-permute-start(bf16[7,128,256]{2,1,0:T(8,128)(2,1)S(1)} %get-tuple-element.20), channel_id=1, source_target_pairs={{0,1},{1,2},{2,3},{3,4},{4,5},{5,6},{6,7},{7,8},{8,9},{9,10},{10,1... | collective-permute-start | bytes 1376264 | tf_op jit(solution)/shard_map/ppermute | solution.py:181
  9.3 0.0 copy-done.9
  9.3 0.0 copy-done.10
  9.3 0.1 copy.15.search
  9.4 4.3 %collective-permute-done.1.after_h = bf16[7,128,256]{2,1,0:T(8,128)(2,1)S(1)} collective-permute-done((bf16[7,128,256]{2,1,0:T(8,128)(2,1)}, bf16[7,128,256]{2,1,0:T(8,128)(2,1)S(1)}, u32[]{:S(2)}, u32[]{:S(2)}) %collective-permute-start.1) | collective-permute-done | bytes 458784 | tf_op jit(solution)/shard_map/ppermute | solution.py:182
  13.7 5.1 %collective-permute-done.before_h = bf16[7,128,256]{2,1,0:T(8,128)(2,1)S(1)} collective-permute-done((bf16[7,128,256]{2,1,0:T(8,128)(2,1)S(1)}, bf16[7,128,256]{2,1,0:T(8,128)(2,1)S(1)}, u32[]{:S(2)}, u32[]{:S(2)}) %collective-permute-start) | collective-permute-done | bytes 458784 | tf_op jit(solution)/shard_map/ppermute | solution.py:181
  18.8 0.0 copy-done.4
  18.8 0.0 copy-done.3
  18.8 0.0 copy-done.1
  18.8 0.0 copy-done.2
  18.8 0.0 copy-done.7
  18.8 0.0 copy-done.6
  18.8 0.0 copy-done.5
  18.8 24.2 %shard_map.139 = (f32[14,128,256]{2,1,0:T(8,128)}, bf16[14,128,256]{2,1,0:T(8,128)(2,1)S(1)}, f32[14,128,128]{2,1,0:T(8,128)S(1)}, f32[14,2,128]{2,1,0:T(2,128)}...) custom-call(s32[14,4]{1,0:T(8,128)S(1)} %copy.15.search, ...), custom_call_target="tpu_custom_call" | custom-call | flops 4697620480 | bytes 10485760 | tf_op jit(solution)/shard_map/pallas_call | solution.py:189
  43.1 4.4 %collective-permute-start.2 = (bf16[7,128,256]{2,1,0:T(8,128)(2,1)S(1)}, bf16[7,128,256]{2,1,0:T(8,128)(2,1)S(1)}, u32[]{:S(2)}, u32[]{:S(2)}) collective-permute-start(bf16[7,128,256]{2,1,0:T(8,128)(2,1)S(1)} %get-tuple-element.15), channel_id=1, source_target_pairs={{0,1},{1,2},{2,3},{3,4},{4,5},{5,6},{6,7},{7,8},{8,9},{9,10},{10,1... | collective-permute-start | bytes 1376264 | tf_op jit(solution)/shard_map/ppermute | solution.py:217
  47.5 1.9 %collective-permute-start.3 = (bf16[7,128,256]{2,1,0:T(8,128)(2,1)S(1)}, bf16[7,128,256]{2,1,0:T(8,128)(2,1)S(1)}, u32[]{:S(2)}, u32[]{:S(2)}) collective-permute-start(bf16[7,128,256]{2,1,0:T(8,128)(2,1)S(1)} %get-tuple-element.16), channel_id=1, source_target_pairs={{1,0},{2,1},{3,2},{4,3},{5,4},{6,5},{7,6},{8,7},{9,8},{10,9},{11,1... | collective-permute-start | bytes 1376264 | tf_op jit(solution)/shard_map/ppermute | solution.py:216
  49.4 0.0 copy-start
  49.4 1.5 %copy-done = f32[14,128,256]{2,1,0:T(8,128)S(1)} copy-done((f32[14,128,256]{2,1,0:T(8,128)S(1)}, f32[14,128,256]{2,1,0:T(8,128)}, u32[]{:S(2)}) %copy-start) | copy-done | bytes 1835032
  50.9 0.0 copy-start.8
  50.9 4.9 %shard_map.140 = f32[14,128,256]{2,1,0:T(8,128)} custom-call(f32[14,128,256]{2,1,0:T(8,128)S(1)} %copy-done, bf16[14,128,256]{2,1,0:T(8,128)(2,1)S(1)} %get-tuple-element.11.mot, f32[14,128,128]{2,1,0:T(8,128)S(1)} %get-tuple-element.12.fcol, bf16[256,512]{1,0:T(8,128)(2,1)S(1)} %copy-done.2, bf16[256,768]{1,0:T(8,128)(2,1)S(1)} %copy-done.1, ...), custom_call_target="tpu_custom_call" | custom-call | flops 1409286144 | bytes 5242880 | tf_op jit(solution)/shard_map/pallas_call | solution.py:220
  55.8 2.0 %collective-permute-done.2 = bf16[7,128,256]{2,1,0:T(8,128)(2,1)S(1)} collective-permute-done((bf16[7,128,256]{2,1,0:T(8,128)(2,1)S(1)}, bf16[7,128,256]{2,1,0:T(8,128)(2,1)S(1)}, u32[]{:S(2)}, u32[]{:S(2)}) %collective-permute-start.2) | collective-permute-done | bytes 458784 | tf_op jit(solution)/shard_map/ppermute | solution.py:217
  57.8 0.0 collective-permute-done.3
  57.8 0.0 copy-done.8
  57.8 0.2 convert_add_fusion.1
  58.0 1.3 %pad_maximum_fusion = f32[14,128,256]{2,1,0:T(8,128)} fusion(f32[7,128,256]{2,1,0:T(8,128)S(1)} %get-tuple-element.18, f32[7,128,256]{2,1,0:T(8,128)S(1)} %get-tuple-element.17), kind=kLoop, calls=%fused_computation | loop fusion | flops 458752 | bytes 3670016 | tf_op jit(solution)/shard_map/concatenate | solution.py:242
  (1 shorter events, 0.0 us)
Async XLA Ops:
  0.6 8.6 %copy-start.9 = (f32[768]{0:T(1024)S(1)}, f32[768]{0:T(1024)}, u32[]{:S(2)}) copy-start(f32[768]{0:T(1024)} %param.23) | copy-start | bytes 9220
  0.6 8.7 %copy-start.10 = (s32[14,4]{0,1:T(4,128)S(1)}, s32[14,4]{0,1:T(4,128)}, u32[]{:S(2)}) copy-start(s32[14,4]{0,1:T(4,128)} %param.16) | copy-start | bytes 676
  0.7 18.1 %copy-start.4 = (f32[2,768]{1,0:T(2,128)S(1)}, f32[2,768]{1,0:T(2,128)}, u32[]{:S(2)}) copy-start(f32[2,768]{1,0:T(2,128)} %disp.3) | copy-start | bytes 18436
  0.7 18.1 %copy-start.3 = (bf16[256,256]{1,0:T(8,128)(2,1)S(1)}, bf16[256,256]{1,0:T(8,128)(2,1)}, u32[]{:S(2)}) copy-start(bf16[256,256]{1,0:T(8,128)(2,1)} %cand_w.3) | copy-start | bytes 393220
  0.7 18.1 %copy-start.1 = (bf16[256,768]{1,0:T(8,128)(2,1)S(1)}, bf16[256,768]{1,0:T(8,128)(2,1)}, u32[]{:S(2)}) copy-start(bf16[256,768]{1,0:T(8,128)(2,1)} %in_w.3) | copy-start | bytes 1179652
  0.7 18.1 %copy-start.2 = (bf16[256,512]{1,0:T(8,128)(2,1)S(1)}, bf16[256,512]{1,0:T(8,128)(2,1)}, u32[]{:S(2)}) copy-start(bf16[256,512]{1,0:T(8,128)(2,1)} %hid_w.3) | copy-start | bytes 786436
  0.7 18.1 %copy-start.7 = (s32[14]{0:T(128)S(1)}, s32[14]{0:T(128)}, u32[]{:S(2)}) copy-start(s32[14]{0:T(128)} %lens.1) | copy-start | bytes 172
  0.7 18.1 %copy-start.6 = (s32[2,14]{1,0:T(2,128)S(1)}, s32[2,14]{1,0:T(2,128)}, u32[]{:S(2)}) copy-start(s32[2,14]{1,0:T(2,128)} %offs.1) | copy-start | bytes 340
  0.7 18.1 %copy-start.5 = (bf16[14,128,256]{2,1,0:T(8,128)(2,1)S(1)}, bf16[14,128,256]{2,1,0:T(8,128)(2,1)}, u32[]{:S(2)}) copy-start(bf16[14,128,256]{2,1,0:T(8,128)(2,1)} %first_h.1) | copy-start | bytes 2752516
  2.8 10.9 %collective-permute-start.1 = (bf16[7,128,256]{2,1,0:T(8,128)(2,1)}, bf16[7,128,256]{2,1,0:T(8,128)(2,1)S(1)}, u32[]{:S(2)}, u32[]{:S(2)}) collective-permute-start(bf16[7,128,256]{2,1,0:T(8,128)(2,1)} %get-tuple-element.19), channel_id=1, source_target_pairs={{1,0},{2,1},{3,2},{4,3},{5,4},{6,5},{7,6},{8,7},{9,8},{10,9},{11,1... | collective-permute-start | bytes 1376264 | tf_op jit(solution)/shard_map/ppermute | solution.py:182
  4.8 14.0 %collective-permute-start = (bf16[7,128,256]{2,1,0:T(8,128)(2,1)S(1)}, bf16[7,128,256]{2,1,0:T(8,128)(2,1)S(1)}, u32[]{:S(2)}, u32[]{:S(2)}) collective-permute-start(bf16[7,128,256]{2,1,0:T(8,128)(2,1)S(1)} %get-tuple-element.20), channel_id=1, source_target_pairs={{0,1},{1,2},{2,3},{3,4},{4,5},{5,6},{6,7},{7,8},{8,9},{9,10},{10,1... | collective-permute-start | bytes 1376264 | tf_op jit(solution)/shard_map/ppermute | solution.py:181
  43.1 14.7 %collective-permute-start.2 = (bf16[7,128,256]{2,1,0:T(8,128)(2,1)S(1)}, bf16[7,128,256]{2,1,0:T(8,128)(2,1)S(1)}, u32[]{:S(2)}, u32[]{:S(2)}) collective-permute-start(bf16[7,128,256]{2,1,0:T(8,128)(2,1)S(1)} %get-tuple-element.15), channel_id=1, source_target_pairs={{0,1},{1,2},{2,3},{3,4},{4,5},{5,6},{6,7},{7,8},{8,9},{9,10},{10,1... | collective-permute-start | bytes 1376264 | tf_op jit(solution)/shard_map/ppermute | solution.py:217
  47.5 10.3 %collective-permute-start.3 = (bf16[7,128,256]{2,1,0:T(8,128)(2,1)S(1)}, bf16[7,128,256]{2,1,0:T(8,128)(2,1)S(1)}, u32[]{:S(2)}, u32[]{:S(2)}) collective-permute-start(bf16[7,128,256]{2,1,0:T(8,128)(2,1)S(1)} %get-tuple-element.16), channel_id=1, source_target_pairs={{1,0},{2,1},{3,2},{4,3},{5,4},{6,5},{7,6},{8,7},{9,8},{10,9},{11,1... | collective-permute-start | bytes 1376264 | tf_op jit(solution)/shard_map/ppermute | solution.py:216
  49.4 1.5 %copy-start = (f32[14,128,256]{2,1,0:T(8,128)S(1)}, f32[14,128,256]{2,1,0:T(8,128)}, u32[]{:S(2)}) copy-start(f32[14,128,256]{2,1,0:T(8,128)} %get-tuple-element.10.h) | copy-start | bytes 5505028
  50.9 6.9 %copy-start.8 = (f32[14,128,256]{2,1,0:T(8,128)S(1)}, f32[14,128,256]{2,1,0:T(8,128)}, u32[]{:S(2)}) copy-start(f32[14,128,256]{2,1,0:T(8,128)} %get-tuple-element.14) | copy-start | bytes 5505028

commit v2 on v1

v2 whole, which is shorter than its diff:
```python
import functools
import math

import jax
import jax.numpy as jnp
from jax import lax
from jax.experimental import pallas as pl
from jax.experimental.pallas import tpu as pltpu
from jax.sharding import PartitionSpec as P

PH = 8
PW = 16
BW = 7
ITERS = 2
GROUP = 2
F32 = jnp.float32
BF16 = jnp.bfloat16
MESH = pl.DeviceIdType.MESH


def dot_nt(a, b):
    return lax.dot_general(a, b, (((1,), (1,)), ((), ())), preferred_element_type=F32)


def dot_tn(a, b):
    return lax.dot_general(a, b, (((0,), (0,)), ((), ())), preferred_element_type=F32)


def sigmoid(x):
    return 0.5 * jnp.tanh(0.5 * x) + 0.5


def gates(h, g, motion, flow_r, flow_c, in_w, cand_w, disp, bias):
    ch = h.shape[1]
    e = jnp.dot(motion, in_w, preferred_element_type=F32)
    e = e + (flow_r * disp[0:1] + (flow_c * disp[1:2] + bias))
    z = sigmoid(g[:, :ch] + e[:, :ch])
    r = sigmoid(g[:, ch:] + e[:, ch : 2 * ch])
    c = jnp.tanh(
        jnp.dot((r * h).astype(BF16), cand_w, preferred_element_type=F32) + e[:, 2 * ch :]
    )
    return h + z * (c - h)


def slot_places(search, offs, refine, b, slots, base, span):
    at = [search[b, l] + offs[refine, b] - base for l in range(slots)]
    return [jnp.minimum(jnp.maximum(i, 0), span - 1) for i in at]


def attention(q, keys, places, length, row_at, col_at):
    slots = len(places)
    cells = q.shape[0]
    scale = 1.0 / math.sqrt(q.shape[1])
    s = dot_nt(q, keys) * scale
    parts = [s[:, l * cells : (l + 1) * cells] for l in range(slots)]
    for l in range(1, slots):
        parts[l] = parts[l] + jnp.where(l < length, 0.0, -1e30).astype(F32)
    top = functools.reduce(jnp.maximum, parts)
    m = jnp.max(top, axis=1, keepdims=True)
    exps = [jnp.exp(p - m) for p in parts]
    total = jnp.sum(functools.reduce(jnp.add, exps), axis=1, keepdims=True)
    inv = 1.0 / total
    w = [x * inv for x in exps]
    half = [x.astype(BF16) for x in w]
    motion = jnp.dot(jnp.concatenate(half, axis=1), keys, preferred_element_type=F32)
    k = lax.broadcasted_iota(jnp.int32, (1, cells), 1)
    ky = (k // PW).astype(F32) / PH
    kx = (k % PW).astype(F32) / PW
    fr = fc = None
    for l in range(slots):
        row = (places[l] * 9363) >> 16
        col = places[l] - row * BW
        y = w[l] * (ky + (row - row_at).astype(F32))
        x = w[l] * (kx + (col - col_at).astype(F32))
        fr, fc = (y, x) if l == 0 else (fr + y, fc + x)
    p = lax.broadcasted_iota(jnp.int32, (cells, 1), 0)
    fr = jnp.sum(fr, axis=1, keepdims=True) - (p // PW).astype(F32) / PH
    fc = jnp.sum(fc, axis=1, keepdims=True) - (p % PW).astype(F32) / PW
    return w, half, motion.astype(BF16), fr, fc


def slot_row_col(b):
    row = (b * 9363) >> 16
    return row + 1, b - row * BW


def main_kernel(
    count, search, offs, lens, prev, last, first_h, second_h, hidden_h, cot_h, hid_h, in_h, cand_h,
    disp, bias,
    hid_out, flow_out, own_out, low_in, high_in,
    win, first, hid0, cot, hid_w, in_w, cand_w, con, hbuf, mot, fcol, gbuf, own, stage,
    sems, out_sems, send_sems, recv_sems,
):
    blocks, cells, ch = first_h.shape
    slots = search.shape[1]
    spare = blocks * slots
    me = lax.axis_index("tile")
    has_prev = me > 0
    has_next = me < count - 1

    barrier = pltpu.get_barrier_semaphore()

    @pl.when(has_prev)
    def _():
        pl.semaphore_signal(barrier, inc=1, device_id={"tile": me - 1}, device_id_type=MESH)

    @pl.when(has_next)
    def _():
        pl.semaphore_signal(barrier, inc=1, device_id={"tile": me + 1}, device_id_type=MESH)

    def local_copy(src, dst, k):
        c = pltpu.make_async_copy(src, dst, sems.at[k])
        c.start()
        return c

    hid_copies = [local_copy(hidden_h, hid0, 0), local_copy(hid_h, hid_w, 1)]

    def remote(src, dst, k, target):
        return pltpu.make_async_remote_copy(
            src_ref=src, dst_ref=dst, send_sem=send_sems.at[k], recv_sem=recv_sems.at[k],
            device_id={"tile": target}, device_id_type=MESH,
        )

    halo_up = remote(second_h.at[pl.ds(blocks - BW, BW)], win.at[pl.ds(0, BW)], 0, me + 1)
    halo_down = remote(second_h.at[pl.ds(0, BW)], win.at[pl.ds(BW + blocks, BW)], 1, me - 1)

    pl.semaphore_wait(barrier, has_prev.astype(jnp.int32) + has_next.astype(jnp.int32))

    @pl.when(has_next)
    def _():
        halo_up.start()

    @pl.when(has_prev)
    def _():
        halo_down.start()

    copies = [
        local_copy(second_h, win.at[pl.ds(BW, blocks)], 2),
        local_copy(first_h, first, 3),
        local_copy(cot_h, cot, 4),
        local_copy(in_h, in_w, 5),
        local_copy(cand_h, cand_w, 6),
    ]
    base = me * blocks - BW
    con[spare] = jnp.zeros((cells, ch), F32)
    for c in hid_copies:
        c.wait()

    def early(b, carry):
        gbuf[b] = jnp.dot(hid0[b], hid_w[...], preferred_element_type=F32)
        return carry

    lax.fori_loop(0, blocks, early, 0)
    for c in copies:
        c.wait()

    @pl.when(has_prev)
    def _():
        halo_up.wait_recv()

    @pl.when(has_next)
    def _():
        halo_down.wait_recv()

    def body(step, carry):
        bs = [step * GROUP + j for j in range(GROUP)]
        at = [slot_row_col(b) for b in bs]
        h = [hid0[b].astype(F32) for b in bs]
        for refine in range(ITERS):
            outs = []
            for j, b in enumerate(bs):
                places = slot_places(search, offs, refine, b, slots, base, win.shape[0])
                keys = jnp.concatenate([win[i] for i in places], axis=0)
                q = (first[b].astype(F32) + h[j]).astype(BF16)
                w, half, motion, fr, fc = attention(q, keys, places, lens[b], *at[j])
                outs.append((motion, fr, fc))
                if refine == ITERS - 1:
                    ct = cot[b]
                    dw = dot_nt(ct, keys)
                    dws = [dw[:, l * cells : (l + 1) * cells] for l in range(slots)]
                    prod = functools.reduce(jnp.add, [w[l] * dws[l] for l in range(slots)])
                    delta = jnp.sum(prod, axis=1, keepdims=True)
                    ds = [
                        (w[l] * (dws[l] - delta) * (1.0 / math.sqrt(ch))).astype(BF16)
                        for l in range(slots)
                    ]
                    stacked = jnp.concatenate(
                        [jnp.concatenate(half, axis=1), jnp.concatenate(ds, axis=1)], axis=0
                    )
                    contrib = dot_tn(stacked, jnp.concatenate([ct, q], axis=0))
                    for l in range(slots):
                        con[b * slots + l] = (
                            contrib[l * cells : (l + 1) * cells] + con[prev[b * slots + l]]
                        )
            if refine < ITERS - 1:
                motion, fr, fc = (jnp.concatenate(t, axis=0) for t in zip(*outs))
                hcat = jnp.concatenate(h, axis=0)
                g = jnp.concatenate([gbuf[b] for b in bs], axis=0)
                hcat = gates(
                    hcat, g, motion, fr, fc, in_w[...], cand_w[...], disp[...], bias[...]
                )
                h = [hcat[j * cells : (j + 1) * cells] for j in range(GROUP)]
            else:
                lane = lax.broadcasted_iota(jnp.int32, (cells, cells), 1)
                for j, b in enumerate(bs):
                    mot[b] = outs[j][0]
                    hbuf[b] = h[j]
                    both = jnp.where(lane == 0, outs[j][1], outs[j][2])
                    fcol[b] = both
                    flow_out[b] = both.T[0:2]
        return carry

    lax.fori_loop(0, blocks // GROUP, body, 0)

    for i in range(BW):
        stage[1, i] = con[last[BW + blocks + i]].astype(BF16)
    grad_up = remote(stage.at[1], low_in, 2, me + 1)

    @pl.when(has_next)
    def _():
        grad_up.start()

    for i in range(BW):
        stage[0, i] = con[last[i]].astype(BF16)
    grad_down = remote(stage.at[0], high_in, 3, me - 1)

    @pl.when(has_prev)
    def _():
        grad_down.start()

    def gather(i, carry):
        own[i] = con[last[BW + i]]
        return carry

    lax.fori_loop(0, blocks, gather, 0)
    own_copy = local_copy(own, own_out, 0)

    def late(step, carry):
        rows = pl.ds(step * GROUP, GROUP)
        h = hbuf[rows].reshape(GROUP * cells, ch)
        f = fcol[rows].reshape(GROUP * cells, cells)
        g = jnp.dot(h.astype(BF16), hid_w[...], preferred_element_type=F32)
        res = gates(
            h, g, mot[rows].reshape(GROUP * cells, ch), f[:, 0:1], f[:, 1:2],
            in_w[...], cand_w[...], disp[...], bias[...],
        )
        hbuf[rows] = res.reshape(GROUP, cells, ch)
        pltpu.make_async_copy(hbuf.at[rows], hid_out.at[rows], out_sems.at[step]).start()
        return carry

    lax.fori_loop(0, blocks // GROUP, late, 0)

    def drain(step, carry):
        rows = pl.ds(step * GROUP, GROUP)
        pltpu.make_async_copy(hbuf.at[rows], hid_out.at[rows], out_sems.at[step]).wait()
        return carry

    lax.fori_loop(0, blocks // GROUP, drain, 0)
    own_copy.wait()

    @pl.when(has_next)
    def _():
        halo_up.wait_send()
        grad_up.wait_send()
        grad_down.wait_recv()

    @pl.when(has_prev)
    def _():
        halo_down.wait_send()
        grad_down.wait_send()
        grad_up.wait_recv()


def local(
    first_feat, second_feat, hidden_init, cotangent, search_list, offsets, lengths,
    hid_weight, in_weight, cand_weight, disp_weight, gate_bias,
):
    blocks, cells, ch = first_feat.shape
    slots = search_list.shape[1]
    n = lax.axis_size("tile")
    me = lax.axis_index("tile")
    span = blocks + 2 * BW
    spare = blocks * slots
    place = (search_list + offsets[ITERS - 1][:, None]).reshape(-1) - me * blocks + BW
    t = jnp.arange(spare, dtype=jnp.int32)
    wanted = jnp.concatenate([place, jnp.arange(span, dtype=jnp.int32)])
    limit = jnp.concatenate([t, jnp.full((span,), spare, jnp.int32)])
    hit = (place[None, :] == wanted[:, None]) & (t[None, :] < limit[:, None])
    found = jnp.max(jnp.where(hit, t[None, :], -1), axis=1)
    found = jnp.where(found < 0, spare, found)
    prev, last = found[:spare], found[spare:]
    bias = gate_bias.reshape(1, -1)
    smem = pl.BlockSpec(memory_space=pltpu.SMEM)
    hbm = pl.BlockSpec(memory_space=pl.ANY)
    vmem = pl.BlockSpec(memory_space=pltpu.VMEM)
    sds = jax.ShapeDtypeStruct
    macs = blocks * cells * (4 * cells * ch * 7 + ch * ch * 12)
    hidden, flow, own, low, high = pl.pallas_call(
        functools.partial(main_kernel, n),
        out_shape=[
            sds((blocks, cells, ch), F32),
            sds((blocks, 2, cells), F32),
            sds((blocks, cells, ch), F32),
            sds((BW, cells, ch), BF16),
            sds((BW, cells, ch), BF16),
        ],
        in_specs=[smem] * 5 + [hbm] * 7 + [vmem] * 2,
        out_specs=[hbm, vmem, hbm, hbm, hbm],
        scratch_shapes=[
            pltpu.VMEM((span, cells, ch), BF16),
            pltpu.VMEM((blocks, cells, ch), BF16),
            pltpu.VMEM((blocks, cells, ch), BF16),
            pltpu.VMEM((blocks, cells, ch), BF16),
            pltpu.VMEM(hid_weight.shape, BF16),
            pltpu.VMEM(in_weight.shape, BF16),
            pltpu.VMEM(cand_weight.shape, BF16),
            pltpu.VMEM((spare + 1, cells, ch), F32),
            pltpu.VMEM((blocks, cells, ch), F32),
            pltpu.VMEM((blocks, cells, ch), BF16),
            pltpu.VMEM((blocks, cells, cells), F32),
            pltpu.VMEM((blocks, cells, 2 * ch), F32),
            pltpu.VMEM((blocks, cells, ch), F32),
            pltpu.VMEM((2, BW, cells, ch), BF16),
            pltpu.SemaphoreType.DMA((7,)),
            pltpu.SemaphoreType.DMA((blocks // GROUP,)),
            pltpu.SemaphoreType.DMA((4,)),
            pltpu.SemaphoreType.DMA((4,)),
        ],
        compiler_params=pltpu.CompilerParams(
            vmem_limit_bytes=52 * 2**20, collective_id=0, has_side_effects=True
        ),
        cost_estimate=pl.CostEstimate(flops=2 * macs, bytes_accessed=10 * 2**20, transcendentals=0),
    )(
        search_list, offsets, lengths, prev, last, first_feat, second_feat,
        hidden_init, cotangent, hid_weight, in_weight, cand_weight, disp_weight, bias,
    )
    from_prev = jnp.where(me > 0, low.astype(F32), 0.0)
    from_next = jnp.where(me < n - 1, high.astype(F32), 0.0)
    own = jnp.concatenate(
        [own[:BW] + from_prev, own[BW : blocks - BW], own[blocks - BW :] + from_next], axis=0
    )
    return hidden, flow, own


def solution(mesh):
    lead = ("grp", "tile")
    return jax.shard_map(
        local,
        mesh=mesh,
        in_specs=(
            P(lead, None, None), P(lead, None, None), P(lead, None, None), P(lead, None, None),
            P(lead, None), P(None, lead), P(lead), P(), P(), P(), P(), P(),
        ),
        out_specs=(P(lead, None, None), P(lead, None, None), P(lead, None, None)),
        check_vma=False,
    )
```

time: 59.6 us -> 58.3 us (0.978)
  Pallas kernels: 29.1 us -> 42.5 us
  starting transfers between devices: 12.7 us -> 0 us
  waiting for transfers between devices: 11.4 us -> 0 us
  local copies, waits for them, and re-layouts: 3.75 us -> 9.9 us
  other arithmetic: 1.56 us -> 4.57 us
    pallas_call x2 -> x1, Pallas kernels: 29.1 us -> 42.5 us  [local(): pl.pallas_call(functools.partial(main_kernel, n), out_shape=[sds((blocks,...]
    ppermute x4 -> x0, starting transfers between devices: 12.7 us -> none  [the longest x1 4.46 us: local(): before = lax.ppermute(second_feat[blocks - BW:], 'tile', up)]
    ppermute x4 -> x0, waiting for transfers between devices: 11.4 us -> none  [the longest x1 5.08 us: local(): before = lax.ppermute(second_feat[blocks - BW:], 'tile', up)]
    unnamed x23 -> x17, local copies, waits for them, and re-layouts: 1.63 us -> 8.28 us
    add x1 -> x2, other arithmetic: 0.22 us -> 2.38 us  [the longest x1 1.7 us: local(): own[:BW] + from_prev]
    slice x1, local copies, waits for them, and re-layouts: 2.12 us -> 0.07 us  [local(): prev, last = (found[:spare], found[spare:])]
    add x0 -> x3, local copies, waits for them, and re-layouts: none -> 0.86 us  [the longest x1 0.68 us: local(): search_list + offsets[ITERS - 1][:, None]]
    reduce_max x0 -> x1, other arithmetic: none -> 0.75 us  [local(): found = jnp.max(jnp.where(hit, t[None, :], -1), axis=1)]
  transfers between devices with their start and end apart: 4 -> 0, of which waited for: 3 -> 0; matrix products, arithmetic and copies ran while one was open for 0% -> 0% of each run, Pallas kernels for 8% -> 0%
where the time goes in v2:
time: 58.3 us; the launch traced here: 57.6 us
  Pallas kernels  42.5 us (73%)
  local copies, waits for them, and re-layouts  9.9 us (17%)
  other arithmetic  4.57 us (8%)
  between operations  0.68 us (1%)
    pallas_call x1, Pallas kernels, local(): pl.pallas_call(functools.partial(main_kernel, n), out_shape=[sds((blocks,...  42.5 us
    unnamed x17, local copies, waits for them, and re-layouts  8.28 us
    add x1, other arithmetic, local(): own[:BW] + from_prev  1.7 us
    concatenate x1, other arithmetic, local(): jnp.concatenate([own[:BW] + from_prev, own[BW:blocks - BW], own[blocks -...  1.35 us

profile of v2, /device:TPU:1, one launch (start us, length us, event | category | flops | bytes accessed | tf_op | source)
XLA Modules:
  0.0 57.6 jit_solution(9551500999063767774)
XLA Ops:
  0.6 0.7 %slice_bitcast_fusion = s32[14]{0:T(128)S(1)} fusion(s32[2,14]{1,0:T(2,128)} %offs.1), kind=kLoop, calls=%fused_computation.9 | loop fusion | bytes 112 | tf_op jit(solution)/shard_map/add | solution.py:284
  1.3 0.7 %subtract_add_fusion = s32[14,4]{0,1:T(4,128)S(1)} fusion(s32[14,4]{0,1:T(4,128)} %param.16, s32[]{:T(128)S(6)} %mul.3, s32[14]{0:T(128)S(1)} %slice_bitcast_fusion), kind=kLoop, calls=%fused_computation.7 | loop fusion | flops 168 | bytes 508 | tf_op jit(solution)/shard_map/add | solution.py:284
  2.0 0.7 %reshape.23.bias = f32[1,768]{1,0:T(1,128)S(1)} reshape(f32[768]{0:T(1024)} %param.23) | data formatting | bytes 6144 | tf_op jit(solution)/shard_map/reshape | solution.py:292
  2.7 0.1 copy.19
  2.8 0.1 add.34
  2.9 0.1 pad_add_fusion
  3.0 0.8 %select_reduce_fusion = s32[84]{0:T(128)S(1)} fusion(s32[84]{0:T(128)} %constant.3.clone.1, s32[84]{0:T(128)S(1)} %pad_add_fusion, s32[56]{0:T(128)S(1)} %add.34), kind=kLoop, calls=%fused_computation.3 | loop fusion | flops 23436 | bytes 1232 | tf_op jit(solution)/shard_map/reduce_max | solution.py:289
  3.7 0.1 slice.17.last
  3.8 0.8 %copy.20.search = s32[14,4]{1,0:T(8,128)S(1)} copy(s32[14,4]{0,1:T(4,128)} %param.16) | data formatting | bytes 448 | tf_op args[4]
  4.6 0.0 copy-start
  4.6 1.0 %copy-done = bf16[256,768]{1,0:T(8,128)(2,1)S(1)} copy-done((bf16[256,768]{1,0:T(8,128)(2,1)S(1)}, bf16[256,768]{1,0:T(8,128)(2,1)}, u32[]{:S(2)}) %copy-start) | copy-done | bytes 393240
  5.6 0.0 copy-start.1
  5.6 0.9 %copy-done.1 = bf16[256,512]{1,0:T(8,128)(2,1)S(1)} copy-done((bf16[256,512]{1,0:T(8,128)(2,1)S(1)}, bf16[256,512]{1,0:T(8,128)(2,1)}, u32[]{:S(2)}) %copy-start.1) | copy-done | bytes 262168
  6.5 0.0 copy-start.2
  6.5 0.9 %copy-done.2 = bf16[256,256]{1,0:T(8,128)(2,1)S(1)} copy-done((bf16[256,256]{1,0:T(8,128)(2,1)S(1)}, bf16[256,256]{1,0:T(8,128)(2,1)}, u32[]{:S(2)}) %copy-start.2) | copy-done | bytes 131096
  7.4 0.0 copy-start.3
  7.4 0.7 %copy-done.3 = f32[2,768]{1,0:T(2,128)S(1)} copy-done((f32[2,768]{1,0:T(2,128)S(1)}, f32[2,768]{1,0:T(2,128)}, u32[]{:S(2)}) %copy-start.3) | copy-done | bytes 6168
  8.1 0.0 copy-start.4
  8.1 0.7 %copy-done.4 = s32[2,14]{1,0:T(2,128)S(1)} copy-done((s32[2,14]{1,0:T(2,128)S(1)}, s32[2,14]{1,0:T(2,128)}, u32[]{:S(2)}) %copy-start.4) | copy-done | bytes 136
  8.8 0.0 copy-start.5
  8.8 0.7 %copy-done.5 = s32[14]{0:T(128)S(1)} copy-done((s32[14]{0:T(128)S(1)}, s32[14]{0:T(128)}, u32[]{:S(2)}) %copy-start.5) | copy-done | bytes 80
  9.4 42.5 %shard_map.139 = (f32[14,128,256]{2,1,0:T(8,128)}, f32[14,2,128]{2,1,0:T(2,128)S(1)}, f32[14,128,256]{2,1,0:T(8,128)}, bf16[7,128,256]{2,1,0:T(8,128)(2,1)S(1)}, bf16[7,128,256]{2,1,0:T(8,128)(2,1)S(1)}) custom-call(s32[14,4]{1,0:T(8,128)S(1)} %copy.20.search, s32[2,14]{1,0:T(2,128)S(1)} %copy-done.4, s32[14]{0:T(128)S(1)} %copy-done.5, s32[56]{0:T(128)S(1)} %bitcast.3, ...), custom_call_target="tpu_custom_call" | custom-call | flops 6106906624 | bytes 10485760 | tf_op jit(solution)/shard_map/pallas_call | solution.py:298
  51.9 1.7 %select_add_fusion.1 = (f32[7,128,256]{2,1,0:T(8,128)S(1)}, f32[7,128,256]{2,1,0:T(8,128)S(1)}) fusion(bf16[7,128,256]{2,1,0:T(8,128)(2,1)S(1)} %get-tuple-element.11, f32[14,128,256]{2,1,0:T(8,128)} %get-tuple-element.10, pred[]{:T(512)S(6)} %gt.3, bf16[7,128,256]{2,1,0:T(8,128)(2,1)S(1)} %get-tuple-element.12, pred[]{:T(512)S(6)} %lt.30), kind=kLoop, calls=%fused_computation.2 | loop fusion | flops 1376256 | bytes 4587522 | tf_op jit(solution)/shard_map/add | solution.py:340
  53.6 0.0 copy-start.6
  53.7 1.3 %pad_maximum_fusion = f32[14,128,256]{2,1,0:T(8,128)} fusion(f32[7,128,256]{2,1,0:T(8,128)S(1)} %get-tuple-element.14, f32[7,128,256]{2,1,0:T(8,128)S(1)} %get-tuple-element.13), kind=kLoop, calls=%fused_computation | loop fusion | flops 458752 | bytes 3670016 | tf_op jit(solution)/shard_map/concatenate | solution.py:339
  55.0 0.8 %copy-done.6 = f32[14,128,256]{2,1,0:T(8,128)S(1)} copy-done((f32[14,128,256]{2,1,0:T(8,128)S(1)}, f32[14,128,256]{2,1,0:T(8,128)}, u32[]{:S(2)}) %copy-start.6) | copy-done | bytes 1835032
  55.8 1.2 %copy.23 = f32[14,128,256]{2,1,0:T(8,128)} copy(f32[14,128,256]{2,1,0:T(8,128)S(1)} %copy-done.6) | data formatting | bytes 3670016
  57.0 0.6 %copy.24 = f32[14,2,128]{2,1,0:T(2,128)} copy(f32[14,2,128]{2,1,0:T(2,128)S(1)} %get-tuple-element.19) | data formatting | bytes 28672
  (2 shorter events, 0.0 us)
Async XLA Ops:
  4.6 1.0 %copy-start = (bf16[256,768]{1,0:T(8,128)(2,1)S(1)}, bf16[256,768]{1,0:T(8,128)(2,1)}, u32[]{:S(2)}) copy-start(bf16[256,768]{1,0:T(8,128)(2,1)} %in_h.1) | copy-start | bytes 1179652
  5.6 0.9 %copy-start.1 = (bf16[256,512]{1,0:T(8,128)(2,1)S(1)}, bf16[256,512]{1,0:T(8,128)(2,1)}, u32[]{:S(2)}) copy-start(bf16[256,512]{1,0:T(8,128)(2,1)} %hid_h.1) | copy-start | bytes 786436
  6.5 0.9 %copy-start.2 = (bf16[256,256]{1,0:T(8,128)(2,1)S(1)}, bf16[256,256]{1,0:T(8,128)(2,1)}, u32[]{:S(2)}) copy-start(bf16[256,256]{1,0:T(8,128)(2,1)} %cand_h.1) | copy-start | bytes 393220
  7.4 0.7 %copy-start.3 = (f32[2,768]{1,0:T(2,128)S(1)}, f32[2,768]{1,0:T(2,128)}, u32[]{:S(2)}) copy-start(f32[2,768]{1,0:T(2,128)} %disp.1) | copy-start | bytes 18436
  8.1 0.7 %copy-start.4 = (s32[2,14]{1,0:T(2,128)S(1)}, s32[2,14]{1,0:T(2,128)}, u32[]{:S(2)}) copy-start(s32[2,14]{1,0:T(2,128)} %offs.1) | copy-start | bytes 340
  8.8 0.7 %copy-start.5 = (s32[14]{0:T(128)S(1)}, s32[14]{0:T(128)}, u32[]{:S(2)}) copy-start(s32[14]{0:T(128)} %lens.1) | copy-start | bytes 172
  53.6 2.2 %copy-start.6 = (f32[14,128,256]{2,1,0:T(8,128)S(1)}, f32[14,128,256]{2,1,0:T(8,128)}, u32[]{:S(2)}) copy-start(f32[14,128,256]{2,1,0:T(8,128)} %get-tuple-element.18) | copy-start | bytes 5505028

commit v3 on v2

--- a/solution.py
+++ b/solution.py
@@ -13,6 +13,7 @@
 BW = 7
 ITERS = 2
 GROUP = 2
+WIDTH = 2
 F32 = jnp.float32
 BF16 = jnp.bfloat16
 MESH = pl.DeviceIdType.MESH
@@ -43,7 +44,7 @@
 
 
 def slot_places(search, offs, refine, b, slots, base, span):
-    at = [search[b, l] + offs[refine, b] - base for l in range(slots)]
+    at = [search[l, b] + offs[refine, b] - base for l in range(slots)]
     return [jnp.minimum(jnp.maximum(i, 0), span - 1) for i in at]
 
 
@@ -88,11 +89,11 @@
     count, search, offs, lens, prev, last, first_h, second_h, hidden_h, cot_h, hid_h, in_h, cand_h,
     disp, bias,
     hid_out, flow_out, own_out, low_in, high_in,
-    win, first, hid0, cot, hid_w, in_w, cand_w, con, hbuf, mot, fcol, gbuf, own, stage,
+    win, front, first, hid0, cot, hid_w, in_w, cand_w, con, hbuf, mot, fcol, gbuf, own, stage,
     sems, out_sems, send_sems, recv_sems,
 ):
     blocks, cells, ch = first_h.shape
-    slots = search.shape[1]
+    slots = search.shape[0]
     spare = blocks * slots
     me = lax.axis_index("tile")
     has_prev = me > 0
@@ -121,14 +122,10 @@
             device_id={"tile": target}, device_id_type=MESH,
         )
 
-    halo_up = remote(second_h.at[pl.ds(blocks - BW, BW)], win.at[pl.ds(0, BW)], 0, me + 1)
+    halo_up = remote(second_h.at[pl.ds(blocks - BW, BW)], front, 0, me + 1)
     halo_down = remote(second_h.at[pl.ds(0, BW)], win.at[pl.ds(BW + blocks, BW)], 1, me - 1)
 
     pl.semaphore_wait(barrier, has_prev.astype(jnp.int32) + has_next.astype(jnp.int32))
-
-    @pl.when(has_next)
-    def _():
-        halo_up.start()
 
     @pl.when(has_prev)
     def _():
@@ -154,16 +151,13 @@
     for c in copies:
         c.wait()
 
-    @pl.when(has_prev)
-    def _():
-        halo_up.wait_recv()
-
     @pl.when(has_next)
     def _():
         halo_down.wait_recv()
-
-    def body(step, carry):
-        bs = [step * GROUP + j for j in range(GROUP)]
+        halo_up.start()
+
+    def body(start, width):
+        bs = [start + j for j in range(width)]
         at = [slot_row_col(b) for b in bs]
         h = [hid0[b].astype(F32) for b in bs]
         for refine in range(ITERS):
@@ -189,17 +183,17 @@
                     )
                     contrib = dot_tn(stacked, jnp.concatenate([ct, q], axis=0))
                     for l in range(slots):
-                        con[b * slots + l] = (
-                            contrib[l * cells : (l + 1) * cells] + con[prev[b * slots + l]]
+                        con[turn_of(b) * slots + l] = (
+                            contrib[l * cells : (l + 1) * cells] + con[prev[l, b]]
                         )
             if refine < ITERS - 1:
                 motion, fr, fc = (jnp.concatenate(t, axis=0) for t in zip(*outs))
                 hcat = jnp.concatenate(h, axis=0)
                 g = jnp.concatenate([gbuf[b] for b in bs], axis=0)
                 hcat = gates(
-                    hcat, g, motion, fr, fc, in_w[...], cand_w[...], disp[...], bias[...]
+                    hcat, g, motion, fr, fc, in_w[...], cand_w[...], disp[...], bias[...].reshape(1, -1)
                 )
-                h = [hcat[j * cells : (j + 1) * cells] for j in range(GROUP)]
+                h = [hcat[j * cells : (j + 1) * cells] for j in range(width)]
             else:
                 lane = lax.broadcasted_iota(jnp.int32, (cells, cells), 1)
                 for j, b in enumerate(bs):
@@ -208,21 +202,33 @@
                     both = jnp.where(lane == 0, outs[j][1], outs[j][2])
                     fcol[b] = both
                     flow_out[b] = both.T[0:2]
-        return carry
-
-    lax.fori_loop(0, blocks // GROUP, body, 0)
-
+
+    def turn_of(b):
+        return b + blocks - BW if isinstance(b, int) and b < BW else b - BW
+
+    def run_row(start):
+        for at in range(start, start + BW, WIDTH):
+            body(at, min(WIDTH, start + BW - at))
+
+    grad_up = remote(stage.at[1], low_in, 2, me + 1)
+    grad_down = remote(stage.at[0], high_in, 3, me - 1)
+
+    run_row(blocks - BW)
     for i in range(BW):
         stage[1, i] = con[last[BW + blocks + i]].astype(BF16)
-    grad_up = remote(stage.at[1], low_in, 2, me + 1)
+
+    @pl.when(has_prev)
+    def _():
+        halo_up.wait_recv()
+        win[0:BW] = front[...]
 
     @pl.when(has_next)
     def _():
         grad_up.start()
 
+    run_row(0)
     for i in range(BW):
         stage[0, i] = con[last[i]].astype(BF16)
-    grad_down = remote(stage.at[0], high_in, 3, me - 1)
 
     @pl.when(has_prev)
     def _():
@@ -242,7 +248,7 @@
         g = jnp.dot(h.astype(BF16), hid_w[...], preferred_element_type=F32)
         res = gates(
             h, g, mot[rows].reshape(GROUP * cells, ch), f[:, 0:1], f[:, 1:2],
-            in_w[...], cand_w[...], disp[...], bias[...],
+            in_w[...], cand_w[...], disp[...], bias[...].reshape(1, -1),
         )
         hbuf[rows] = res.reshape(GROUP, cells, ch)
         pltpu.make_async_copy(hbuf.at[rows], hid_out.at[rows], out_sems.at[step]).start()
@@ -281,17 +287,20 @@
     me = lax.axis_index("tile")
     span = blocks + 2 * BW
     spare = blocks * slots
-    place = (search_list + offsets[ITERS - 1][:, None]).reshape(-1) - me * blocks + BW
-    t = jnp.arange(spare, dtype=jnp.int32)
-    wanted = jnp.concatenate([place, jnp.arange(span, dtype=jnp.int32)])
-    limit = jnp.concatenate([t, jnp.full((span,), spare, jnp.int32)])
-    hit = (place[None, :] == wanted[:, None]) & (t[None, :] < limit[:, None])
-    found = jnp.max(jnp.where(hit, t[None, :], -1), axis=1)
-    found = jnp.where(found < 0, spare, found)
-    prev, last = found[:spare], found[spare:]
-    bias = gate_bias.reshape(1, -1)
+    listed = search_list.T
+    place = listed + offsets[ITERS - 1][None, :] - me * blocks + BW
+    slot = lax.broadcasted_iota(jnp.int32, (slots, blocks), 0)
+    order = lax.broadcasted_iota(jnp.int32, (slots, blocks), 1)
+    turn = jnp.where(order < BW, order + blocks - BW, order - BW) * slots + slot
+    earlier = turn[None, None] < turn[:, :, None, None]
+    same = (place[None, None] == place[:, :, None, None]) & earlier
+    prev = jnp.max(jnp.where(same, turn[None, None], -1), axis=(2, 3))
+    prev = jnp.where(prev < 0, spare, prev)
+    hit = place[None] == lax.broadcasted_iota(jnp.int32, (span, 1, 1), 0)
+    last = jnp.max(jnp.where(hit, turn[None], -1), axis=(1, 2))
+    last = jnp.where(last < 0, spare, last)
     smem = pl.BlockSpec(memory_space=pltpu.SMEM)
-    hbm = pl.BlockSpec(memory_space=pl.ANY)
+    hbm = pl.BlockSpec(memory_space=pltpu.HBM)
     vmem = pl.BlockSpec(memory_space=pltpu.VMEM)
     sds = jax.ShapeDtypeStruct
     macs = blocks * cells * (4 * cells * ch * 7 + ch * ch * 12)
@@ -308,6 +317,7 @@
         out_specs=[hbm, vmem, hbm, hbm, hbm],
         scratch_shapes=[
             pltpu.VMEM((span, cells, ch), BF16),
+            pltpu.VMEM((BW, cells, ch), BF16),
             pltpu.VMEM((blocks, cells, ch), BF16),
             pltpu.VMEM((blocks, cells, ch), BF16),
             pltpu.VMEM((blocks, cells, ch), BF16),
@@ -327,12 +337,12 @@
             pltpu.SemaphoreType.DMA((4,)),
         ],
         compiler_params=pltpu.CompilerParams(
-            vmem_limit_bytes=52 * 2**20, collective_id=0, has_side_effects=True
+            vmem_limit_bytes=60 * 2**20, collective_id=0, has_side_effects=True
         ),
         cost_estimate=pl.CostEstimate(flops=2 * macs, bytes_accessed=10 * 2**20, transcendentals=0),
     )(
-        search_list, offsets, lengths, prev, last, first_feat, second_feat,
-        hidden_init, cotangent, hid_weight, in_weight, cand_weight, disp_weight, bias,
+        listed, offsets, lengths, prev, last, first_feat, second_feat,
+        hidden_init, cotangent, hid_weight, in_weight, cand_weight, disp_weight, gate_bias,
     )
     from_prev = jnp.where(me > 0, low.astype(F32), 0.0)
     from_next = jnp.where(me < n - 1, high.astype(F32), 0.0)

time: 58.3 us -> 46 us (0.79)
  the two profiles are of different devices: /device:TPU:1 before, /device:TPU:23 now
where the time goes in v3:
time: 46 us; the launch traced here: 45.8 us
  Pallas kernels  35.1 us (76%)
  other arithmetic  6.46 us (14%)
  local copies, waits for them, and re-layouts  3.51 us (8%)
  between operations  0.67 us (1%)
    pallas_call x1, Pallas kernels, local(): pl.pallas_call(functools.partial(main_kernel, n), out_shape=[sds((blocks,...  35.1 us
    unnamed x6, local copies, waits for them, and re-layouts  2.64 us
    add x1, other arithmetic, local(): own[:BW] + from_prev  1.91 us
    concatenate x1, other arithmetic, local(): jnp.concatenate([own[:BW] + from_prev, own[BW:blocks - BW], own[blocks -...  1.35 us
    reduce_max x1, other arithmetic, local(): prev = jnp.max(jnp.where(same, turn[None, None], -1), axis=(2, 3))  1.21 us

profile of v3, /device:TPU:23, one launch (start us, length us, event | category | flops | bytes accessed | tf_op | source)
XLA Modules:
  0.0 45.8 jit_solution(18310565153360809663)
XLA Ops:
  0.6 0.7 %slice_bitcast_fusion = s32[14]{0:T(128)S(1)} fusion(s32[2,14]{1,0:T(2,128)} %offs.1), kind=kLoop, calls=%fused_computation.13 | loop fusion | bytes 112 | tf_op jit(solution)/shard_map/add | solution.py:291
  1.3 0.7 %subtract_add_fusion = s32[4,14]{1,0:T(4,128)S(1)} fusion(s32[]{:T(128)S(6)} %mul.25, s32[14]{0:T(128)S(1)} %slice_bitcast_fusion, s32[14,4]{0,1:T(4,128)} %param.16), kind=kLoop, calls=%fused_computation.9 | loop fusion | flops 168 | bytes 508 | tf_op jit(solution)/shard_map/add | solution.py:291
  2.0 0.1 iota_add_fusion
  2.1 0.1 copy.15
  2.2 1.2 %select_reduce_fusion = s32[4,14]{1,0:T(4,128)S(1)} fusion(s32[4,14]{1,0:T(4,128)S(1)} %copy.15, s32[4,14]{1,0:T(4,128)S(1)} %subtract_add_fusion), kind=kLoop, calls=%fused_computation.3 | loop fusion | flops 15624 | bytes 672 | tf_op jit(solution)/shard_map/reduce_max | solution.py:297
  3.4 0.6 %compare_select_fusion.prev = s32[4,14]{1,0:T(4,128)} fusion(s32[4,14]{1,0:T(4,128)S(1)} %select_reduce_fusion), kind=kLoop, calls=%fused_computation.7 | loop fusion | flops 112 | bytes 448 | tf_op jit(solution)/shard_map/jit(_where)/select_n | solution.py:298
  4.0 0.1 copy.17
  4.1 0.1 select_reduce_fusion.1
  4.2 0.5 %compare_select_fusion.1.last = s32[28]{0:T(128)} fusion(s32[28]{0:T(128)S(1)} %select_reduce_fusion.1), kind=kLoop, calls=%fused_computation.8 | loop fusion | flops 56 | bytes 224 | tf_op jit(solution)/shard_map/jit(_where)/select_n | solution.py:301
  4.7 35.1 %shard_map.139 = (f32[14,128,256]{2,1,0:T(8,128)}, f32[14,2,128]{2,1,0:T(2,128)}, f32[14,128,256]{2,1,0:T(8,128)}, bf16[7,128,256]{2,1,0:T(8,128)(2,1)}, bf16[7,128,256]{2,1,0:T(8,128)(2,1)}) custom-call(s32[4,14]{1,0:T(4,128)} %bitcast.4, s32[2,14]{1,0:T(2,128)} %offs.1, s32[14]{0:T(128)} %lens.1, s32[4,14]{1,0:T(4,128)} %compare_select_fusion.prev, ...), custom_call_target="tpu_custom_call" | custom-call | flops 6106906624 | bytes 10485760 | tf_op jit(solution)/shard_map/pallas_call | solution.py:307
  39.9 1.9 %select_add_fusion.1 = (f32[7,128,256]{2,1,0:T(8,128)S(1)}, f32[7,128,256]{2,1,0:T(8,128)S(1)}) fusion(bf16[7,128,256]{2,1,0:T(8,128)(2,1)} %get-tuple-element.11, f32[14,128,256]{2,1,0:T(8,128)} %get-tuple-element.10, pred[]{:T(512)S(6)} %gt.3, bf16[7,128,256]{2,1,0:T(8,128)(2,1)} %get-tuple-element.12, pred[]{:T(512)S(6)} %lt.42), kind=kLoop, calls=%fused_computation.2 | loop fusion | flops 1376256 | bytes 4587522 | tf_op jit(solution)/shard_map/add | solution.py:350
  41.8 0.0 copy-start
  41.8 1.3 %pad_maximum_fusion = f32[14,128,256]{2,1,0:T(8,128)} fusion(f32[7,128,256]{2,1,0:T(8,128)S(1)} %get-tuple-element.14, f32[7,128,256]{2,1,0:T(8,128)S(1)} %get-tuple-element.13), kind=kLoop, calls=%fused_computation | loop fusion | flops 458752 | bytes 3670016 | tf_op jit(solution)/shard_map/concatenate | solution.py:349
  43.1 0.8 %copy-done = f32[14,128,256]{2,1,0:T(8,128)S(1)} copy-done((f32[14,128,256]{2,1,0:T(8,128)S(1)}, f32[14,128,256]{2,1,0:T(8,128)}, u32[]{:S(2)}) %copy-start) | copy-done | bytes 1835032
  43.9 0.0 copy-start.1
  43.9 1.2 %copy.20 = f32[14,128,256]{2,1,0:T(8,128)} copy(f32[14,128,256]{2,1,0:T(8,128)S(1)} %copy-done) | data formatting | bytes 3670016
  45.2 0.0 copy-done.1
  45.2 0.6 %copy.21 = f32[14,2,128]{2,1,0:T(2,128)} copy(f32[14,2,128]{2,1,0:T(2,128)S(1)} %copy-done.1) | data formatting | bytes 28672
  (2 shorter events, 0.0 us)
Async XLA Ops:
  41.8 2.2 %copy-start = (f32[14,128,256]{2,1,0:T(8,128)S(1)}, f32[14,128,256]{2,1,0:T(8,128)}, u32[]{:S(2)}) copy-start(f32[14,128,256]{2,1,0:T(8,128)} %get-tuple-element.20) | copy-start | bytes 5505028
  43.9 1.2 %copy-start.1 = (f32[14,2,128]{2,1,0:T(2,128)S(1)}, f32[14,2,128]{2,1,0:T(2,128)}, u32[]{:S(2)}) copy-start(f32[14,2,128]{2,1,0:T(2,128)} %get-tuple-element.21) | copy-start | bytes 43012
